TPU v7x, 512 devices: a whole 4x8x8 slice. The times are simulated.
512 devices in a mesh: blk: 32 (over y, x_lo, core), col: 16 (over x_hi, z).
Axes of the slice: x: 4 (x_hi: 2, x_lo: 2; x = x_hi * 2 + x_lo), y: 8, z: 8, core: 2. Of those that a mesh axis runs over, the one named last changes fastest.
Arguments:
- features: bfloat16 [65536, 768], P(('blk', 'col')), may hold values from -24 to 24
- node_order: int32 [512, 128], P(('blk', 'col')), may hold values from 0 to 127, each once within a row
- weight: bfloat16 [768, 256], replicated, may hold values from -0.21875 to 0.21875
- cotangent: bfloat16 [65536, 256], P(('blk', 'col')), may hold values from -6 to 6
- tile_list: int32 [49152, 2], P(('blk', 'col')), may hold values from -1 to 511, as said below
- tile_values: bfloat16 [49152, 128, 128], P(('blk', 'col')), may hold values from -0.078125 to 0.078125
Outputs:
- hidden: bfloat16 [65536, 256], P(('blk', 'col'))
- x_grad: bfloat16 [65536, 768], P(('blk', 'col'))
- weight_grad: float32 [768, 256], replicated
Inputs may be any that keep to these rules, and one draw needn't show every extreme that they name: `tile_list`: slots held by one device come in groups of 3, group g taking tiles whose column block is among the 1 block that device (blk index g, the holder's col index) holds. A live slot's row block is among the 16 blocks of the holder's blk index; an empty slot has row block -1 and a valid column block. Every device has at least one full group.
All inputs are finite; a program needn't handle non-finite values.
Results may differ from a plain program's by a relative error of at most 0.0075.
Values may be sent and summed in bfloat16 or wider, within the bound.
No kernel may reach another device: no remote copies, remote signals or barrier semaphores. Data moves between devices by JAX's collectives and lax.ppermute only.
A program may use at most 128 MiB of HBM per device.

v0:
```python
import jax
import jax.numpy as jnp
from jax import lax
from jax.sharding import PartitionSpec as P

SLOTS = 3


def shifted(value, axis, steps):
    count = lax.axis_size(axis)
    pairs = [(source, (source + steps) % count) for source in range(count)]
    return lax.ppermute(value, axis, pairs)


def gelu_tanh(values):
    return jax.nn.gelu(values, approximate=True)


def gelu_backward(values, upstream):
    _, pull = jax.vjp(gelu_tanh, values)
    return pull(upstream.astype(jnp.float32))[0].astype(jnp.bfloat16)


def per_device(features, node_order, weight, cotangent, tile_list, tile_values):
    tile_size = tile_values.shape[1]
    hidden_width = weight.shape[1]
    in_width = weight.shape[0]
    own_blocks = node_order.shape[0]
    col_count = lax.axis_size("col")
    blk_count = lax.axis_size("blk")
    range_blocks = own_blocks * col_count
    own_rows = own_blocks * tile_size
    lanes = jnp.arange(tile_size, dtype=jnp.int32)
    order_onehot = (node_order[:, :, None] == lanes[None, None, :]).astype(jnp.bfloat16)
    feature_blocks = features.reshape(own_blocks, tile_size, in_width)
    reordered = jnp.einsum(
        "qik,qkf->qif", order_onehot, feature_blocks, preferred_element_type=jnp.float32
    )
    reordered = reordered.astype(jnp.bfloat16).reshape(own_rows, in_width)
    panel = jnp.dot(reordered, weight, preferred_element_type=jnp.float32).astype(jnp.bfloat16)
    row_ids = tile_list[:, 0]
    col_ids = tile_list[:, 1]
    row_local = jnp.where(row_ids >= 0, row_ids % range_blocks, -1)
    row_target = jnp.where(row_ids >= 0, row_ids % range_blocks, range_blocks)
    col_local = col_ids % own_blocks
    range_ids = jnp.arange(range_blocks, dtype=jnp.int32)
    row_select = (row_local[:, None] == range_ids[None, :]).astype(jnp.bfloat16)
    empty = jnp.zeros((range_blocks + 1, tile_size, hidden_width), jnp.float32)
    piece = lax.all_gather(panel, "blk", axis=0, tiled=True)
    group_count = piece.shape[0] // own_rows
    slot_count = group_count * SLOTS
    part_tiles = tile_values
    part_cols = col_local
    part_rows = row_target
    position = jnp.arange(slot_count, dtype=jnp.int32) // SLOTS * own_blocks + part_cols
    piece_blocks = piece.reshape(group_count * own_blocks, tile_size, hidden_width)
    picked = jnp.take(piece_blocks, position, axis=0)
    product = jnp.einsum("sij,sjf->sif", part_tiles, picked, preferred_element_type=jnp.float32)
    partial_value = empty.at[part_rows].add(product)
    partial_value = partial_value[:range_blocks].reshape(range_blocks * tile_size, hidden_width)
    own_agg = lax.psum_scatter(partial_value, "col", scatter_dimension=0, tiled=True)
    hidden = gelu_tanh(own_agg).astype(jnp.bfloat16)
    own_grad = gelu_backward(own_agg, cotangent)
    grad_range = lax.all_gather(own_grad, "col", axis=0, tiled=True)
    grad_blocks = grad_range.reshape(range_blocks, tile_size, hidden_width)

    def contribution(group, width):
        part_tiles = lax.dynamic_slice_in_dim(tile_values, group * SLOTS, SLOTS, 0)
        part_rows = lax.dynamic_slice_in_dim(row_select, group * SLOTS, SLOTS, 0)
        part_cols = lax.dynamic_slice_in_dim(col_local, group * SLOTS, SLOTS, 0)
        grad_sel = jnp.einsum(
            "sr,rif->sif", part_rows, grad_blocks, preferred_element_type=jnp.float32
        )
        grad_sel = grad_sel.astype(jnp.bfloat16)
        product = jnp.einsum(
            "sij,sif->sjf", part_tiles, grad_sel, preferred_element_type=jnp.float32
        )
        placed = jnp.zeros((own_blocks, tile_size, width), jnp.float32).at[part_cols].add(product)
        return placed.reshape(own_rows, width)

    blk_here = lax.axis_index("blk")
    grad_total = contribution(jnp.mod(blk_here - 1, blk_count), hidden_width)

    def cycle_single(turn, carried):
        carried = shifted(carried, "blk", 1)
        return carried + contribution(jnp.mod(blk_here - turn - 1, blk_count), hidden_width)

    grad_total = lax.fori_loop(1, blk_count, cycle_single, grad_total)
    panel_grad = grad_total.astype(jnp.bfloat16)
    weight_term = lax.dot_general(
        reordered, panel_grad, (((0,), (0,)), ((), ())), preferred_element_type=jnp.float32
    )
    node_total = own_rows * col_count * blk_count
    weight_grad = lax.psum(weight_term, ("blk", "col")) * node_total ** (-0.5)
    row_grad = lax.dot_general(
        panel_grad, weight, (((1,), (1,)), ((), ())), preferred_element_type=jnp.float32
    )
    row_grad = row_grad.astype(jnp.bfloat16).reshape(own_blocks, tile_size, in_width)
    x_grad = jnp.einsum("qik,qif->qkf", order_onehot, row_grad, preferred_element_type=jnp.float32)
    x_grad = x_grad.astype(jnp.bfloat16).reshape(own_rows, in_width)
    return (hidden, x_grad, weight_grad)


def solution(mesh):
    in_specs = (
        P(("blk", "col"), None),
        P(("blk", "col"), None),
        P(),
        P(("blk", "col"), None),
        P(("blk", "col"), None),
        P(("blk", "col"), None, None),
    )
    out_specs = (P(("blk", "col"), None), P(("blk", "col"), None), P())
    return jax.shard_map(
        per_device, mesh=mesh, in_specs=in_specs, out_specs=out_specs, check_vma=False
    )
```

profile of v0, /device:TPU:1, one launch (start us, length us, event | category | flops | bytes accessed | tf_op | source)
XLA Modules:
  0.0 972.1 jit_solution(1375954454679516254)
XLA Ops:
  11.5 72.3 %all-gather.3.cloned.1.call-done = bf16[4096,256]{1,0:T(8,128)(2,1)} async-done(((bf16[128,256]{1,0:T(8,128)(2,1)}), bf16[4096,256]{1,0:T(8,128)(2,1)}) %all-gather.3.cloned.1.call-update) | async-done | bytes 2097168 | tf_op jit(solution)/shard_map/all_gather | solution.py:49
  83.8 7.7 gather_fusion
  91.5 9.3 fusion.11
  100.8 12.6 %copy.13 = f32[96,128,256]{2,1,0:T(8,128)} copy(f32[96,128,256]{1,2,0:T(8,128)} %fusion.11) | data formatting | bytes 25165824 | tf_op jit(solution)/shard_map/sij,sjf->sif/dot_general | solution.py:58
  113.6 18.3 %scatter_fusion.1 = f32[17,128,256]{2,1,0:T(8,128)S(1)} fusion(f32[17,128,256]{2,1,0:T(8,128)S(1)} %broadcast_in_dim.30, s32[96]{0:T(128)S(1)} %fusion.42, f32[96,128,256]{2,1,0:T(8,128)} %copy.13), kind=kCustom, calls=%fused_computation.2 | custom fusion | flops 3145728 | bytes 37749120 | tf_op jit(solution)/shard_map/scatter-add | solution.py:59
  133.5 205.3 %reduce-scatter.2.cloned.1.call-done = f32[128,256]{1,0:T(8,128)} async-done(((f32[2048,256]{1,0:T(8,128)}), f32[128,256]{1,0:T(8,128)}) %reduce-scatter.2.cloned.1.call-update) | async-done | bytes 131088 | tf_op jit(solution)/shard_map/reduce_scatter | solution.py:61
  340.6 4.6 copy.14
  345.2 80.6 %all-gather.5.cloned.1.call-done = bf16[2048,256]{1,0:T(8,128)(2,1)} async-done(((bf16[128,256]{1,0:T(8,128)(2,1)}), bf16[2048,256]{1,0:T(8,128)(2,1)}) %all-gather.5.cloned.1.call-update) | async-done | bytes 1048592 | tf_op jit(solution)/shard_map/all_gather | solution.py:64
  425.9 2.0 fusion.15
  429.9 260.1 %while.15 = (s32[]{:T(128)}, f32[128,256]{1,0:T(8,128)S(1)}, s32[]{:T(128)}, bf16[96,128,128]{1,2,0:T(8,128)(2,1)}, bf16[96,16]{0,1:T(8,128)(2,1)S(1)}, /*index=...) while((s32[]{:T(128)}, f32[128,256]{1,0:T(8,128)S(1)}, ...), condition=%wide.region_5.6_spmd, body=%wide.region_3.5_spmd.sunk | while | flops 28442644 | bytes 4165000 | solution.py:88
  429.9 6.6 collective-permute-start
  439.4 3.5 collective-permute-start
  445.7 3.5 collective-permute-start
  452.0 2.1 collective-permute-done
  454.1 1.9 collective-permute-start
  458.8 3.7 collective-permute-done
  462.5 1.9 collective-permute-start
  467.2 3.7 collective-permute-done
  471.0 1.9 collective-permute-start
  475.6 3.7 collective-permute-done
  479.4 1.9 collective-permute-start
  484.1 3.7 collective-permute-done
  487.8 1.9 collective-permute-start
  492.5 3.7 collective-permute-done
  496.2 1.9 collective-permute-start
  500.9 3.7 collective-permute-done
  504.7 1.9 collective-permute-start
  509.4 3.7 collective-permute-done
  513.1 1.9 collective-permute-start
  517.8 3.7 collective-permute-done
  521.5 1.9 collective-permute-start
  526.2 3.7 collective-permute-done
  530.0 1.9 collective-permute-start
  534.6 3.7 collective-permute-done
  538.4 1.9 collective-permute-start
  543.1 3.7 collective-permute-done
  546.8 1.9 collective-permute-start
  551.5 3.7 collective-permute-done
  555.2 1.9 collective-permute-start
  559.9 3.7 collective-permute-done
  563.7 1.9 collective-permute-start
  568.3 3.7 collective-permute-done
  572.1 1.9 collective-permute-start
  576.8 3.7 collective-permute-done
  580.5 1.9 collective-permute-start
  585.2 3.7 collective-permute-done
  589.0 1.9 collective-permute-start
  593.6 3.7 collective-permute-done
  597.4 1.9 collective-permute-start
  602.1 3.7 collective-permute-done
  610.5 3.7 collective-permute-done
  618.9 3.7 collective-permute-done
  627.3 3.7 collective-permute-done
  631.1 1.9 collective-permute-start
  635.8 3.7 collective-permute-done
  644.2 3.7 collective-permute-done
  652.6 3.7 collective-permute-done
  661.0 3.7 collective-permute-done
  664.8 1.9 collective-permute-start
  669.5 3.7 collective-permute-done
  677.9 3.7 collective-permute-done
  686.3 3.7 collective-permute-done
  692.4 271.0 %all-reduce.2.cloned.1.call-done = f32[768,256]{1,0:T(8,128)} async-done(((f32[768,256]{1,0:T(8,128)}), f32[768,256]{1,0:T(8,128)}) %all-reduce.2.cloned.1.call-update) | async-done | bytes 786448 | tf_op jit(solution)/shard_map/psum | solution.py:94
  963.5 2.1 broadcast_multiply_fusion
  (235 shorter events, 111.3 us)
Async XLA Ops:
  7.2 2.0 copy-start
  7.2 76.6 %all-gather.3.cloned.1.call-start = ((), (), s32[]{:S(2)}) async-start(), calls=%async_computation.1 | async-start | bytes 2162688 | tf_op jit(solution)/shard_map/all_gather | solution.py:49
  8.5 0.7 copy-start.3
  10.0 328.8 %reduce-scatter.2.cloned.1.call-start = ((), (), s32[]{:S(2)}) async-start(), calls=%async_computation.2 | async-start | bytes 2228224 | tf_op jit(solution)/shard_map/reduce_scatter | solution.py:61
  83.8 7.7 copy-start.2
  131.9 207.0 %copy-start.5 = (bf16[128,256]{1,0:T(8,128)(2,1)S(1)}, bf16[128,256]{1,0:T(8,128)(2,1)}, u32[]{:S(2)}) copy-start(bf16[128,256]{1,0:T(8,128)(2,1)} %param.11) | copy-start | bytes 196612
  133.4 292.4 %all-gather.5.cloned.1.call-start = ((), (), s32[]{:S(2)}) async-start(), calls=%async_computation.3 | async-start | bytes 1114112 | tf_op jit(solution)/shard_map/all_gather | solution.py:64
  340.5 623.0 %all-reduce.2.cloned.1.call-start = ((), (), s32[]{:S(2)}) async-start(), calls=%async_computation.4 | async-start | bytes 1572864 | tf_op jit(solution)/shard_map/psum | solution.py:94
  425.9 4.0 copy-start.1
  429.9 260.2 %copy-start.4 = (bf16[128,768]{1,0:T(8,128)(2,1)S(1)}, bf16[128,768]{1,0:T(8,128)(2,1)}, u32[]{:S(2)}) copy-start(bf16[128,768]{1,0:T(8,128)(2,1)} %copy-done.3) | copy-start | bytes 589828
  429.9 261.4 %copy-start.6 = (s32[1,128]{1,0:T(1,128)S(1)}, s32[1,128]{1,0:T(1,128)}, u32[]{:S(2)}) copy-start(s32[1,128]{1,0:T(1,128)} %param.9) | copy-start | bytes 1540
  429.9 9.4 collective-permute-start
  439.4 6.3 collective-permute-start
  445.7 8.4 collective-permute-start
  454.1 8.4 collective-permute-start
  462.5 8.4 collective-permute-start
  471.0 8.4 collective-permute-start
  479.4 8.4 collective-permute-start
  487.8 8.4 collective-permute-start
  496.2 8.4 collective-permute-start
  504.7 8.4 collective-permute-start
  513.1 8.4 collective-permute-start
  521.5 8.4 collective-permute-start
  530.0 8.4 collective-permute-start
  538.4 8.4 collective-permute-start
  546.8 8.4 collective-permute-start
  555.2 8.4 collective-permute-start
  563.7 8.4 collective-permute-start
  572.1 8.4 collective-permute-start
  580.5 8.4 collective-permute-start
  589.0 8.4 collective-permute-start
  597.4 8.4 collective-permute-start
  605.8 8.4 collective-permute-start
  614.2 8.4 collective-permute-start
  622.7 8.4 collective-permute-start
  631.1 8.4 collective-permute-start
  639.5 8.4 collective-permute-start
  648.0 8.4 collective-permute-start
  656.4 8.4 collective-permute-start
  664.8 8.4 collective-permute-start
  673.2 8.4 collective-permute-start
  681.7 8.4 collective-permute-start
Sparse Core Ops, SparseCore 0:
  10.7 72.9 all-gather.2
  133.6 205.2 reduce-scatter.1
  342.6 83.2 all-gather.4
  691.4 272.0 all-reduce.1
where the time goes:
time: 975 us; the launch traced here: 972 us
  waiting for transfers between devices  736 us (75%)
  matrix products  73.2 us (8%)
  starting transfers between devices  67.6 us (7%)
  other arithmetic  51.2 us (5%)
  local copies, waits for them, and re-layouts  27.8 us (3%)
  between operations  13.9 us (1%)
    psum x1, waiting for transfers between devices, per_device(): weight_grad = lax.psum(weight_term, ('blk', 'col')) * node_total ** (-0.5)  271 us
    reduce_scatter x1, waiting for transfers between devices, per_device(): lax.psum_scatter(partial_value, 'col', scatter_dimension=0, tiled=True)  205 us
    ppermute x31, waiting for transfers between devices, shifted(): return lax.ppermute(value, axis, pairs)  106 us
    all_gather x1, waiting for transfers between devices, per_device(): grad_range = lax.all_gather(own_grad, 'col', axis=0, tiled=True)  80.6 us
    all_gather x1, waiting for transfers between devices, per_device(): piece = lax.all_gather(panel, 'blk', axis=0, tiled=True)  72.3 us
    ppermute x31, starting transfers between devices, shifted(): return lax.ppermute(value, axis, pairs)  67.4 us
    dot_general x32, matrix products, contribution(): jnp.einsum('sij,sif->sjf', part_tiles, grad_sel, preferred_element_type=j...  34.7 us
    scatter-add x32, other arithmetic, contribution(): jnp.zeros((own_blocks, tile_size, width), jnp.float32).at[part_cols]  27.3 us
  transfers between devices with their start and end apart: 35, of which 33 were waited for; matrix products, arithmetic and copies ran while one was open for 9% of the time, Pallas kernels for 0%

commit v1 on v0

v1 whole, which is shorter than its diff:
```python
import functools

import jax
import jax.numpy as jnp
from jax import lax
from jax.experimental import pallas as pl
from jax.experimental.pallas import tpu as pltpu
from jax.sharding import Mesh
from jax.sharding import PartitionSpec as P

AXES = ("y", "xl", "core", "xh", "z")
CHIPS = ("y", "xl")
COLS = ("xh", "z")
SWAP = [(0, 1), (1, 0)]
VMEM = pl.BlockSpec(memory_space=pltpu.VMEM)
SMEM = pl.BlockSpec(memory_space=pltpu.SMEM)
F32 = jnp.float32
BF16 = jnp.bfloat16


def swap(value):
    return lax.ppermute(value, "core", SWAP)


def exchange(value, axes):
    return lax.all_to_all(value, axes, 0, 0, tiled=True)


def params(mib):
    return pltpu.CompilerParams(vmem_limit_bytes=mib * 1024 * 1024)


def dot(a, b, contract):
    return lax.dot_general(a, b, (contract, ((), ())), preferred_element_type=F32)


def source_onehot(order):
    size = order.shape[1]
    rows = lax.broadcasted_iota(jnp.int32, (size, size), 0)
    return (rows == order).astype(F32).astype(BF16)


def panel_kernel(core, order, features, weight, mine, theirs):
    half = mine.shape[1]
    whole = dot(features[...], weight[...], ((1,), (0,))).astype(BF16)
    whole = dot(source_onehot(order[...]), whole, ((0,), (0,))).astype(BF16)
    left, right = whole[:, :half], whole[:, half:]
    first = core[0] == 0
    mine[...] = jnp.where(first, left, right)
    theirs[...] = jnp.where(first, right, left)


def forward_kernel(core, rows_own, rows_other, panels, own, other, out, total):
    chips = panels.shape[0]
    size = panels.shape[2]
    ranges = out.shape[0]
    slots = own.shape[0] // (2 * chips)
    total[...] = jnp.zeros_like(total)
    me = core[0]

    def one_chip(chip, carry):
        for bit in range(2):
            group = 2 * chip + bit
            panel = panels[chip, bit ^ me]
            for which, (tiles, rows) in enumerate(((own, rows_own), (other, rows_other))):
                stack = tiles[pl.ds(group * slots, slots)].reshape(slots * size, size)
                product = dot(stack, panel, ((1,), (0,)))
                for slot in range(slots):
                    row = rows[group * slots + slot]
                    place = which * (ranges + 1) + row
                    total[place] += product[slot * size:(slot + 1) * size]
        return carry

    lax.fori_loop(0, chips, one_chip, 0)
    for which in range(2):
        base = which * (ranges + 1)
        out[:, which] = total[base:base + ranges].astype(BF16)


def middle_kernel(parts, cotangent, hidden, grad):
    scale = (2.0 / jnp.pi) ** 0.5
    for which in range(2):
        agg = jnp.sum(parts[:, which].astype(F32), axis=0)
        square = agg * agg
        slope = scale * (1.0 + 3.0 * 0.044715 * square)
        bend = jnp.tanh(scale * (agg + 0.044715 * (agg * square)))
        cdf = 0.5 * (1.0 + bend)
        hidden[which] = (agg * cdf).astype(BF16)
        upstream = cotangent[which].astype(F32)
        derivative = cdf + agg * (0.5 * (1.0 - bend * bend) * slope)
        turned = (upstream * derivative).T.astype(BF16)
        grad[:, which] = jnp.broadcast_to(turned[None], (grad.shape[0],) + turned.shape)


def backward_kernel(core, rows_own, rows_other, grads, own, other, out):
    chips = out.shape[0]
    size = grads.shape[2]
    ranges = grads.shape[0]
    slots = own.shape[0] // (2 * chips)
    me = core[0]

    def one_chip(chip, carry):
        for bit in range(2):
            group = 2 * chip + bit
            lefts = []
            rights = []
            for which, (tiles, rows) in enumerate(((own, rows_own), (other, rows_other))):
                for slot in range(slots):
                    row = rows[group * slots + slot]
                    block = grads[jnp.minimum(row, ranges - 1), which]
                    lefts.append(jnp.where(row < ranges, block, jnp.zeros_like(block)))
                rights.append(tiles[pl.ds(group * slots, slots)].reshape(slots * size, size))
            left = jnp.concatenate(lefts, axis=1)
            right = jnp.concatenate(rights, axis=0)
            out[chip, bit ^ me] = dot(left, right, ((1,), (0,))).astype(BF16)
        return carry

    lax.fori_loop(0, chips, one_chip, 0)


def weight_kernel(scale, parts, order_own, order_other, own, other, turned, term):
    total = 0.0
    for which, (order, features) in enumerate(((order_own, own), (order_other, other))):
        panel_grad = jnp.sum(parts[:, which].astype(F32), axis=0).astype(BF16)
        placed = dot(panel_grad, source_onehot(order[...]), ((1,), (1,))).astype(BF16)
        turned[which] = placed
        total = total + dot(placed, features[...], ((1,), (0,)))
    term[...] = (total * scale).T.astype(BF16)


def feature_kernel(core, mine, theirs, weight, out):
    half = mine.shape[0]
    me = core[0]
    near = weight[:, pl.ds(pl.multiple_of(me * half, half), half)]
    far = weight[:, pl.ds(pl.multiple_of((1 - me) * half, half), half)]
    total = dot(mine[...], near, ((0,), (1,))) + dot(theirs[...], far, ((0,), (1,)))
    out[...] = total.astype(BF16)


def per_device(features, node_order, weight, cotangent, tile_list, tile_values):
    tiles, size, _ = tile_values.shape
    in_width, hid = weight.shape
    half = hid // 2
    chips = lax.axis_size("y") * lax.axis_size("xl")
    ranges = lax.axis_size("xh") * lax.axis_size("z")
    nodes = 2 * chips * ranges * size
    core = lax.axis_index("core").astype(jnp.int32).reshape(1)
    first = core[0] == 0

    def halves(value):
        left, right = value[:, :half], value[:, half:]
        return jnp.where(first, left, right), jnp.where(first, right, left)

    def joined(near, far):
        return jnp.where(
            first, jnp.concatenate([near, far], 1), jnp.concatenate([far, near], 1)
        )

    mine, theirs = pl.pallas_call(
        panel_kernel,
        out_shape=[jax.ShapeDtypeStruct((size, half), BF16)] * 2,
        in_specs=[SMEM, VMEM, VMEM, VMEM],
        out_specs=[VMEM] * 2,
        compiler_params=params(16),
    )(core, node_order, features, weight)
    pair = jnp.stack([mine, swap(theirs)])
    panels = exchange(jnp.broadcast_to(pair[None], (chips, 2, size, half)), CHIPS)

    row_ids = tile_list[:, 0]
    rows_own = jnp.where(row_ids >= 0, row_ids % ranges, ranges)
    rows_other = swap(rows_own)
    tiles_other = swap(tile_values)
    order_other = swap(node_order)
    features_other = swap(features)
    near_cot, far_cot = halves(cotangent)
    cot_pair = jnp.stack([near_cot, swap(far_cot)])

    partial = pl.pallas_call(
        forward_kernel,
        out_shape=jax.ShapeDtypeStruct((ranges, 2, size, half), BF16),
        in_specs=[SMEM, SMEM, SMEM, VMEM, VMEM, VMEM],
        out_specs=VMEM,
        scratch_shapes=[pltpu.VMEM((2 * (ranges + 1), size, half), F32)],
        compiler_params=params(24),
    )(core, rows_own, rows_other, panels, tile_values, tiles_other)
    parts = exchange(partial, COLS)
    hidden_pair, grad = pl.pallas_call(
        middle_kernel,
        out_shape=[
            jax.ShapeDtypeStruct((2, size, half), BF16),
            jax.ShapeDtypeStruct((ranges, 2, half, size), BF16),
        ],
        in_specs=[VMEM] * 2,
        out_specs=[VMEM] * 2,
        compiler_params=params(16),
    )(parts, cot_pair)
    grads = exchange(grad, COLS)
    hidden = joined(hidden_pair[0], swap(hidden_pair[1]))

    contribution = pl.pallas_call(
        backward_kernel,
        out_shape=jax.ShapeDtypeStruct((chips, 2, half, size), BF16),
        in_specs=[SMEM, SMEM, SMEM, VMEM, VMEM, VMEM],
        out_specs=VMEM,
        compiler_params=params(24),
    )(core, rows_own, rows_other, grads, tile_values, tiles_other)
    parts = exchange(contribution, CHIPS)
    turned, term = pl.pallas_call(
        functools.partial(weight_kernel, nodes ** -0.5),
        out_shape=[
            jax.ShapeDtypeStruct((2, half, size), BF16),
            jax.ShapeDtypeStruct((in_width, half), BF16),
        ],
        in_specs=[VMEM] * 5,
        out_specs=[VMEM] * 2,
        compiler_params=params(16),
    )(parts, node_order, order_other, features, features_other)

    def summed(value):
        return jnp.sum(value.astype(F32), axis=0).astype(BF16)

    share = in_width // ranges
    term = summed(exchange(term.reshape(ranges, share, half), COLS))
    term = summed(exchange(jnp.broadcast_to(term[None], (chips, share, half)), CHIPS))
    term = exchange(jnp.broadcast_to(term[None], (ranges, share, half)), COLS)
    term = term.reshape(in_width, half)
    weight_grad = joined(term, swap(term)).astype(F32)

    x_grad = pl.pallas_call(
        feature_kernel,
        out_shape=jax.ShapeDtypeStruct((size, in_width), BF16),
        in_specs=[SMEM, VMEM, VMEM, VMEM],
        out_specs=VMEM,
        compiler_params=params(16),
    )(core, turned[0], swap(turned[1]), weight)
    return (hidden, x_grad, weight_grad)


def solution(mesh):
    blk, col = mesh.devices.shape
    fine = Mesh(mesh.devices.reshape(blk // 4, 2, 2, 2, col // 2), AXES)
    rows = P(AXES)
    return jax.shard_map(
        per_device,
        mesh=fine,
        in_specs=(rows, rows, P(), rows, rows, rows),
        out_specs=(rows, rows, P()),
        check_vma=False,
    )
```

time: 975 us -> 223 us (0.23)
  waiting for transfers between devices: 736 us -> 63.7 us
  matrix products: 73.2 us -> 0 us
  blocking collectives: 0 us -> 63.2 us
  other arithmetic: 51.2 us -> 1.76 us
  local copies, waits for them, and re-layouts: 27.8 us -> 6.61 us
  Pallas kernels: 0 us -> 16.3 us
  between operations: 13.9 us -> 0.91 us
    psum x1 -> x0, waiting for transfers between devices: 271 us -> none  [per_device(): weight_grad = lax.psum(weight_term, ('blk', 'col')) * node_total ** (-0.5)]
    reduce_scatter x1 -> x0, waiting for transfers between devices: 205 us -> none  [per_device(): lax.psum_scatter(partial_value, 'col', scatter_dimension=0, tiled=True)]
    all_gather x2 -> x0, waiting for transfers between devices: 153 us -> none  [the longest x1 80.6 us: per_device(): grad_range = lax.all_gather(own_grad, 'col', axis=0, tiled=True)]
    ppermute x31 -> x9, waiting for transfers between devices: 106 us -> 4.56 us  [swap(): return lax.ppermute(value, 'core', SWAP)]
    dot_general x69 -> x0, matrix products: 73.2 us -> none  [the longest x32 34.7 us: contribution(): jnp.einsum('sij,sif->sjf', part_tiles, grad_sel, preferred_element_type=j...]
    all_to_all x0 -> x3, blocking collectives: none -> 63.2 us  [exchange(): return lax.all_to_all(value, axes, 0, 0, tiled=True)]
    all_to_all x0 -> x4, waiting for transfers between devices: none -> 59.1 us  [exchange(): return lax.all_to_all(value, axes, 0, 0, tiled=True)]
    scatter-add x33 -> x0, other arithmetic: 45.6 us -> none  [the longest x32 27.3 us: contribution(): jnp.zeros((own_blocks, tile_size, width), jnp.float32).at[part_cols]]
  transfers between devices with their start and end apart: 35 -> 13, of which waited for: 33 -> 9; matrix products, arithmetic and copies ran while one was open for 9% -> 1% of each run, Pallas kernels for 0% -> 1%
where the time goes in v1:
time: 223 us; the launch traced here: 222 us
  starting transfers between devices  70 us (31%)
  waiting for transfers between devices  63.7 us (29%)
  blocking collectives  63.2 us (28%)
  Pallas kernels  16.3 us (7%)
  local copies, waits for them, and re-layouts  6.61 us (3%)
    all_to_all x3, blocking collectives, exchange(): return lax.all_to_all(value, axes, 0, 0, tiled=True)  63.2 us
    all_to_all x4, waiting for transfers between devices, exchange(): return lax.all_to_all(value, axes, 0, 0, tiled=True)  59.1 us
    ppermute x9, starting transfers between devices, swap(): return lax.ppermute(value, 'core', SWAP)  39.5 us
    all_to_all x4, starting transfers between devices, exchange(): return lax.all_to_all(value, axes, 0, 0, tiled=True)  30.5 us
    pallas_call x1, Pallas kernels, per_device(): pl.pallas_call(forward_kernel, out_shape=jax.ShapeDtypeStruct((ranges, 2,...  6.76 us
    pallas_call x1, Pallas kernels, per_device(): pl.pallas_call(backward_kernel, out_shape=jax.ShapeDtypeStruct((chips, 2,...  6.04 us
    unnamed x22, local copies, waits for them, and re-layouts  4.61 us
    ppermute x9, waiting for transfers between devices, swap(): return lax.ppermute(value, 'core', SWAP)  4.56 us
  transfers between devices with their start and end apart: 13, of which 9 were waited for; matrix products, arithmetic and copies ran while one was open for 1% of the time, Pallas kernels for 1%

profile of v1, /device:TPU:1, one launch (start us, length us, event | category | flops | bytes accessed | tf_op | source)
XLA Modules:
  0.0 222.5 jit_solution(15391493773882784326)
XLA Ops:
  0.6 0.0 copy-start
  0.6 9.1 %collective-permute-start.2 = (bf16[96,128,128]{2,1,0:T(8,128)(2,1)}, bf16[96,128,128]{2,1,0:T(8,128)(2,1)}, u32[]{:S(2)}, u32[]{:S(2)}) collective-permute-start(bf16[96,128,128]{2,1,0:T(8,128)(2,1)} %own.4), channel_id=1, source_target_pairs={{0,16},{16,0},{1,17},{17,1},{2,18},{18,2},{3,19},{19,3},{4,20},{20... | collective-permute-start | bytes 9437192 | tf_op jit(solution)/shard_map/ppermute | solution.py:22
  9.7 0.0 copy-start.3
  9.7 1.0 copy-done.3
  10.7 0.0 copy-start.5
  10.7 0.9 copy-done.5
  11.6 0.0 copy-start.7
  11.6 0.7 copy-done.7
  12.3 0.0 copy-start.10
  12.3 0.4 shard_map.85
  12.7 1.9 collective-permute-start.1
  14.6 1.2 collective-permute-done.1
  15.8 1.3 broadcast_in_dim.8
  17.0 4.3 %all-to-all-start = ((bf16[16,2,128,128]{3,2,1,0:T(8,128)(2,1)}), bf16[16,2,128,128]{3,2,1,0:T(8,128)(2,1)}, u32[]{:S(2)}, u32[]{:S(2)}) async-start(bf16[16,2,128,128]{3,2,1,0:T(8,128)(2,1)} %broadcast_in_dim.8), calls=%async_computation | async-start | bytes 2097152 | tf_op jit(solution)/shard_map/all_to_all | solution.py:26
  21.4 0.0 copy-done.10
  21.4 0.0 copy-start.9
  21.4 2.2 collective-permute-start
  23.6 0.9 collective-permute-done.rows_other
  24.6 23.6 %all-to-all-done.panels = bf16[16,2,128,128]{3,2,1,0:T(8,128)(2,1)} async-done(((bf16[16,2,128,128]{3,2,1,0:T(8,128)(2,1)}), bf16[16,2,128,128]{3,2,1,0:T(8,128)(2,1)}, u32[]{:S(2)}, u32[]{:S(2)}) %all-to-all-start) | async-done | bytes 1048608 | tf_op jit(solution)/shard_map/all_to_all | solution.py:26
  48.1 0.0 collective-permute-done.2.other
  48.1 0.0 copy-done
  48.1 6.8 %shard_map.86 = bf16[16,2,128,128]{3,2,1,0:T(8,128)(2,1)S(1)} custom-call(s32[1]{0:T(128)} %bitcast.core, s32[96]{0:T(128)S(1)} %compare_select_fusion.2.rows_own, s32[96]{0:T(128)S(1)} %collective-permute-done.rows_other, bf16[16,2,128,128]{3,2,1,0:T(8,128)(2,1)} %all-to-all-done.panels, bf16[96,128,128]{2,1,0:T(8,128)(2,1)S(1)} %copy-done, ...), custom_call_target="tpu_custom_call" | custom-call | tf_op jit(solution)/shard_map/pallas_call | solution.py:178
  54.9 0.0 copy-start.1
  54.9 1.0 copy-done.1
  55.9 9.8 %all-to-all-start.1 = ((bf16[16,2,128,128]{3,2,1,0:T(8,128)(2,1)}), bf16[16,2,128,128]{3,2,1,0:T(8,128)(2,1)}, u32[]{:S(2)}, u32[]{:S(2)}) async-start(bf16[16,2,128,128]{3,2,1,0:T(8,128)(2,1)} %copy-done.1), calls=%async_computation.1 | async-start | bytes 2097152 | tf_op jit(solution)/shard_map/all_to_all | solution.py:26
  65.7 0.0 copy-done.9
  65.8 6.0 %collective-permute-start.3 = (bf16[128,128]{1,0:T(8,128)(2,1)S(1)}, bf16[128,128]{1,0:T(8,128)(2,1)S(1)}, u32[]{:S(2)}, u32[]{:S(2)}) collective-permute-start(bf16[128,128]{1,0:T(8,128)(2,1)S(1)} %get-tuple-element.20), channel_id=1, source_target_pairs={{0,16},{16,0},{1,17},{17,1},{2,18},{18,2},{3,19},{19,3},{4,20},{20... | collective-permute-start | bytes 98312 | tf_op jit(solution)/shard_map/ppermute | solution.py:22
  71.7 0.8 collective-permute-done.3
  72.6 15.8 %all-to-all-done.1.parts = bf16[16,2,128,128]{3,2,1,0:T(8,128)(2,1)} async-done(((bf16[16,2,128,128]{3,2,1,0:T(8,128)(2,1)}), bf16[16,2,128,128]{3,2,1,0:T(8,128)(2,1)}, u32[]{:S(2)}, u32[]{:S(2)}) %all-to-all-start.1) | async-done | bytes 1048608 | tf_op jit(solution)/shard_map/all_to_all | solution.py:26
  88.3 1.6 shard_map.87
  90.0 31.5 %all_to_all.35.grads = bf16[16,2,128,128]{3,2,1,0:T(8,128)(2,1)S(1)} all-to-all(bf16[16,2,128,128]{3,2,1,0:T(8,128)(2,1)S(1)} %get-tuple-element.12), channel_id=1, replica_groups=mesh['y'=8,'xl'=2,'core'=2,'xh'=2,'z'=8] {'xh','z'}, dimensions={0} | all-to-all | bytes 2097152 | tf_op jit(solution)/shard_map/all_to_all | solution.py:26
  121.4 0.0 copy-start.6
  121.4 0.0 copy-start.8
  121.4 6.0 %shard_map.88 = bf16[16,2,128,128]{3,2,1,0:T(8,128)(2,1)S(1)} custom-call(s32[1]{0:T(128)} %bitcast.core, s32[96]{0:T(128)S(1)} %compare_select_fusion.2.rows_own, s32[96]{0:T(128)S(1)} %collective-permute-done.rows_other, bf16[16,2,128,128]{3,2,1,0:T(8,128)(2,1)S(1)} %all_to_all.35.grads, bf16[96,128,128]{2,1,0:T(8,128)(2,1)S(1)} %copy-done, ...), custom_call_target="tpu_custom_call" | custom-call | tf_op jit(solution)/shard_map/pallas_call | solution.py:200
  127.5 0.0 copy-start.2
  127.5 1.0 copy-done.2
  128.5 0.0 copy-start.4
  128.5 10.8 %all-to-all-start.3 = ((bf16[16,2,128,128]{3,2,1,0:T(8,128)(2,1)}), bf16[16,2,128,128]{3,2,1,0:T(8,128)(2,1)S(1)}, u32[]{:S(2)}, u32[]{:S(2)}) async-start(bf16[16,2,128,128]{3,2,1,0:T(8,128)(2,1)} %copy-done.2), calls=%async_computation.3 | async-start | bytes 2097152 | tf_op jit(solution)/shard_map/all_to_all | solution.py:26
  139.3 0.0 copy-done.6
  139.3 5.4 %collective-permute-start.6 = (bf16[128,768]{1,0:T(8,128)(2,1)S(1)}, bf16[128,768]{1,0:T(8,128)(2,1)S(1)}, u32[]{:S(2)}, u32[]{:S(2)}) collective-permute-start(bf16[128,768]{1,0:T(8,128)(2,1)S(1)} %copy-done.6), channel_id=1, source_target_pairs={{0,16},{16,0},{1,17},{17,1},{2,18},{18,2},{3,19},{19,3},{4,20},{20... | collective-permute-start | bytes 589832 | tf_op jit(solution)/shard_map/ppermute | solution.py:22
  144.7 0.0 copy-done.8
  144.7 1.9 collective-permute-start.5
  146.6 1.1 collective-permute-done.5.order_other
  147.7 0.0 collective-permute-done.6.other
  147.7 15.8 %all-to-all-done.3.parts = bf16[16,2,128,128]{3,2,1,0:T(8,128)(2,1)S(1)} async-done(((bf16[16,2,128,128]{3,2,1,0:T(8,128)(2,1)}), bf16[16,2,128,128]{3,2,1,0:T(8,128)(2,1)S(1)}, u32[]{:S(2)}, u32[]{:S(2)}) %all-to-all-start.3) | async-done | bytes 1048608 | tf_op jit(solution)/shard_map/all_to_all | solution.py:26
  163.4 0.6 shard_map.89
  164.0 16.5 %all_to_all.36 = bf16[16,48,128]{2,1,0:T(8,128)(2,1)S(1)} all-to-all(bf16[16,48,128]{2,1,0:T(8,128)(2,1)S(1)} %bitcast.18), channel_id=1, replica_groups=mesh['y'=8,'xl'=2,'core'=2,'xh'=2,'z'=8] {'xh','z'}, dimensions={0} | all-to-all | bytes 393216 | tf_op jit(solution)/shard_map/all_to_all | solution.py:26
  180.6 15.2 %all_to_all.37 = bf16[16,48,128]{2,1,0:T(8,128)(2,1)S(1)} all-to-all(bf16[16,48,128]{2,1,0:T(8,128)(2,1)S(1)} %broadcast_in_dim.9), channel_id=1, replica_groups=mesh['y'=8,'xl'=2,'core'=2,'xh'=2,'z'=8] {'y','xl'}, dimensions={0} | all-to-all | bytes 393216 | tf_op jit(solution)/shard_map/all_to_all | solution.py:26
  195.9 0.7 broadcast_in_dim.10
  196.6 5.6 %all-to-all-start.6 = ((bf16[16,48,128]{2,1,0:T(8,128)(2,1)}), bf16[16,48,128]{2,1,0:T(8,128)(2,1)S(1)}, u32[]{:S(2)}, u32[]{:S(2)}) async-start(bf16[16,48,128]{2,1,0:T(8,128)(2,1)} %broadcast_in_dim.10), calls=%async_computation.6 | async-start | bytes 393216 | tf_op jit(solution)/shard_map/all_to_all | solution.py:26
  202.2 5.0 %collective-permute-start.4 = (bf16[128,128]{1,0:T(8,128)(2,1)S(1)}, bf16[128,128]{1,0:T(8,128)(2,1)S(1)}, u32[]{:S(2)}, u32[]{:S(2)}) collective-permute-start(bf16[128,128]{1,0:T(8,128)(2,1)S(1)} %get-tuple-element.18), channel_id=1, source_target_pairs={{0,16},{16,0},{1,17},{17,1},{2,18},{18,2},{3,19},{19,3},{4,20},{20... | collective-permute-start | bytes 98312 | tf_op jit(solution)/shard_map/ppermute | solution.py:22
  207.1 4.0 %all-to-all-done.6 = bf16[16,48,128]{2,1,0:T(8,128)(2,1)S(1)} async-done(((bf16[16,48,128]{2,1,0:T(8,128)(2,1)}), bf16[16,48,128]{2,1,0:T(8,128)(2,1)S(1)}, u32[]{:S(2)}, u32[]{:S(2)}) %all-to-all-start.6) | async-done | bytes 196640 | tf_op jit(solution)/shard_map/all_to_all | solution.py:26
  211.1 6.2 %collective-permute-start.8 = (bf16[768,128]{1,0:T(8,128)(2,1)S(1)}, bf16[768,128]{1,0:T(8,128)(2,1)S(1)}, u32[]{:S(2)}, u32[]{:S(2)}) collective-permute-start(bf16[768,128]{1,0:T(8,128)(2,1)S(1)} %bitcast.20), channel_id=1, source_target_pairs={{0,16},{16,0},{1,17},{17,1},{2,18},{18,2},{3,19},{19,3},{4,20},{20... | collective-permute-start | bytes 589832 | tf_op jit(solution)/shard_map/ppermute | solution.py:22
  217.4 1.9 collective-permute-start.7
  219.3 0.0 collective-permute-done.4
  219.3 0.6 maximum_select_fusion.1
  220.0 0.5 collective-permute-done.7.theirs
  220.5 0.0 copy-done.4
  220.5 1.0 shard_map.90
  221.5 0.0 collective-permute-done.8
  221.5 1.0 fusion
  (9 shorter events, 0.1 us)
Async XLA Ops:
  0.6 47.5 %copy-start = (bf16[96,128,128]{2,1,0:T(8,128)(2,1)S(1)}, bf16[96,128,128]{2,1,0:T(8,128)(2,1)}, u32[]{:S(2)}) copy-start(bf16[96,128,128]{2,1,0:T(8,128)(2,1)} %own.4) | copy-start | bytes 9437188
  0.6 47.5 %collective-permute-start.2 = (bf16[96,128,128]{2,1,0:T(8,128)(2,1)}, bf16[96,128,128]{2,1,0:T(8,128)(2,1)}, u32[]{:S(2)}, u32[]{:S(2)}) collective-permute-start(bf16[96,128,128]{2,1,0:T(8,128)(2,1)} %own.4), channel_id=1, source_target_pairs={{0,16},{16,0},{1,17},{17,1},{2,18},{18,2},{3,19},{19,3},{4,20},{20... | collective-permute-start | bytes 9437192 | tf_op jit(solution)/shard_map/ppermute | solution.py:22
  9.7 1.0 copy-start.3
  10.7 0.9 copy-start.5
  11.6 0.7 copy-start.7
  12.3 9.1 %copy-start.10 = (s32[96,2]{0,1:T(2,128)S(1)}, s32[96,2]{0,1:T(2,128)}, u32[]{:S(2)}) copy-start(s32[96,2]{0,1:T(2,128)} %param.10) | copy-start | bytes 2308
  12.7 3.1 %collective-permute-start.1 = (bf16[128,128]{1,0:T(8,128)(2,1)S(1)}, bf16[128,128]{1,0:T(8,128)(2,1)S(1)}, u32[]{:S(2)}, u32[]{:S(2)}) collective-permute-start(bf16[128,128]{1,0:T(8,128)(2,1)S(1)} %get-tuple-element.10), channel_id=1, source_target_pairs={{0,16},{16,0},{1,17},{17,1},{2,18},{18,2},{3,19},{19,3},{4,20},{20... | collective-permute-start | bytes 98312 | tf_op jit(solution)/shard_map/ppermute | solution.py:22
  17.0 31.1 %all-to-all-start = ((bf16[16,2,128,128]{3,2,1,0:T(8,128)(2,1)}), bf16[16,2,128,128]{3,2,1,0:T(8,128)(2,1)}, u32[]{:S(2)}, u32[]{:S(2)}) async-start(bf16[16,2,128,128]{3,2,1,0:T(8,128)(2,1)} %broadcast_in_dim.8), calls=%async_computation | async-start | bytes 2097152 | tf_op jit(solution)/shard_map/all_to_all | solution.py:26
  21.4 44.3 %copy-start.9 = (bf16[128,256]{1,0:T(8,128)(2,1)S(1)}, bf16[128,256]{1,0:T(8,128)(2,1)}, u32[]{:S(2)}) copy-start(bf16[128,256]{1,0:T(8,128)(2,1)} %param.9) | copy-start | bytes 196612
  21.4 3.1 %collective-permute-start = (s32[96]{0:T(128)S(1)}, s32[96]{0:T(128)S(1)}, u32[]{:S(2)}, u32[]{:S(2)}) collective-permute-start(s32[96]{0:T(128)S(1)} %compare_select_fusion.2.rows_own), channel_id=1, source_target_pairs={{0,16},{16,0},{1,17},{17,1},{2,18},{18,2},{3,19},{19,3},{4,20},{20... | collective-permute-start | bytes 1160 | tf_op jit(solution)/shard_map/ppermute | solution.py:22
  54.9 1.0 copy-start.1
  55.9 32.4 %all-to-all-start.1 = ((bf16[16,2,128,128]{3,2,1,0:T(8,128)(2,1)}), bf16[16,2,128,128]{3,2,1,0:T(8,128)(2,1)}, u32[]{:S(2)}, u32[]{:S(2)}) async-start(bf16[16,2,128,128]{3,2,1,0:T(8,128)(2,1)} %copy-done.1), calls=%async_computation.1 | async-start | bytes 2097152 | tf_op jit(solution)/shard_map/all_to_all | solution.py:26
  65.8 6.8 %collective-permute-start.3 = (bf16[128,128]{1,0:T(8,128)(2,1)S(1)}, bf16[128,128]{1,0:T(8,128)(2,1)S(1)}, u32[]{:S(2)}, u32[]{:S(2)}) collective-permute-start(bf16[128,128]{1,0:T(8,128)(2,1)S(1)} %get-tuple-element.20), channel_id=1, source_target_pairs={{0,16},{16,0},{1,17},{17,1},{2,18},{18,2},{3,19},{19,3},{4,20},{20... | collective-permute-start | bytes 98312 | tf_op jit(solution)/shard_map/ppermute | solution.py:22
  121.4 17.9 %copy-start.6 = (bf16[128,768]{1,0:T(8,128)(2,1)S(1)}, bf16[128,768]{1,0:T(8,128)(2,1)}, u32[]{:S(2)}) copy-start(bf16[128,768]{1,0:T(8,128)(2,1)} %own.5) | copy-start | bytes 589828
  121.4 23.2 %copy-start.8 = (s32[1,128]{1,0:T(1,128)S(1)}, s32[1,128]{1,0:T(1,128)}, u32[]{:S(2)}) copy-start(s32[1,128]{1,0:T(1,128)} %order_own.1) | copy-start | bytes 1540
  127.5 1.0 copy-start.2
  128.5 92.0 %copy-start.4 = (bf16[768,256]{1,0:T(8,128)(2,1)S(1)}, bf16[768,256]{1,0:T(8,128)(2,1)}, u32[]{:S(2)}) copy-start(bf16[768,256]{1,0:T(8,128)(2,1)} %weight.3) | copy-start | bytes 1179652
  128.5 35.0 %all-to-all-start.3 = ((bf16[16,2,128,128]{3,2,1,0:T(8,128)(2,1)}), bf16[16,2,128,128]{3,2,1,0:T(8,128)(2,1)S(1)}, u32[]{:S(2)}, u32[]{:S(2)}) async-start(bf16[16,2,128,128]{3,2,1,0:T(8,128)(2,1)} %copy-done.2), calls=%async_computation.3 | async-start | bytes 2097152 | tf_op jit(solution)/shard_map/all_to_all | solution.py:26
  139.3 8.4 %collective-permute-start.6 = (bf16[128,768]{1,0:T(8,128)(2,1)S(1)}, bf16[128,768]{1,0:T(8,128)(2,1)S(1)}, u32[]{:S(2)}, u32[]{:S(2)}) collective-permute-start(bf16[128,768]{1,0:T(8,128)(2,1)S(1)} %copy-done.6), channel_id=1, source_target_pairs={{0,16},{16,0},{1,17},{17,1},{2,18},{18,2},{3,19},{19,3},{4,20},{20... | collective-permute-start | bytes 589832 | tf_op jit(solution)/shard_map/ppermute | solution.py:22
  144.7 3.0 %collective-permute-start.5 = (s32[1,128]{1,0:T(1,128)S(1)}, s32[1,128]{1,0:T(1,128)S(1)}, u32[]{:S(2)}, u32[]{:S(2)}) collective-permute-start(s32[1,128]{1,0:T(1,128)S(1)} %copy-done.8), channel_id=1, source_target_pairs={{0,16},{16,0},{1,17},{17,1},{2,18},{18,2},{3,19},{19,3},{4,20},{20... | collective-permute-start | bytes 1544 | tf_op jit(solution)/shard_map/ppermute | solution.py:22
  196.6 14.5 %all-to-all-start.6 = ((bf16[16,48,128]{2,1,0:T(8,128)(2,1)}), bf16[16,48,128]{2,1,0:T(8,128)(2,1)S(1)}, u32[]{:S(2)}, u32[]{:S(2)}) async-start(bf16[16,48,128]{2,1,0:T(8,128)(2,1)} %broadcast_in_dim.10), calls=%async_computation.6 | async-start | bytes 393216 | tf_op jit(solution)/shard_map/all_to_all | solution.py:26
  202.2 17.2 %collective-permute-start.4 = (bf16[128,128]{1,0:T(8,128)(2,1)S(1)}, bf16[128,128]{1,0:T(8,128)(2,1)S(1)}, u32[]{:S(2)}, u32[]{:S(2)}) collective-permute-start(bf16[128,128]{1,0:T(8,128)(2,1)S(1)} %get-tuple-element.18), channel_id=1, source_target_pairs={{0,16},{16,0},{1,17},{17,1},{2,18},{18,2},{3,19},{19,3},{4,20},{20... | collective-permute-start | bytes 98312 | tf_op jit(solution)/shard_map/ppermute | solution.py:22
  211.1 10.3 %collective-permute-start.8 = (bf16[768,128]{1,0:T(8,128)(2,1)S(1)}, bf16[768,128]{1,0:T(8,128)(2,1)S(1)}, u32[]{:S(2)}, u32[]{:S(2)}) collective-permute-start(bf16[768,128]{1,0:T(8,128)(2,1)S(1)} %bitcast.20), channel_id=1, source_target_pairs={{0,16},{16,0},{1,17},{17,1},{2,18},{18,2},{3,19},{19,3},{4,20},{20... | collective-permute-start | bytes 589832 | tf_op jit(solution)/shard_map/ppermute | solution.py:22
  217.4 3.1 %collective-permute-start.7 = (bf16[128,128]{1,0:T(8,128)(2,1)S(1)}, bf16[128,128]{1,0:T(8,128)(2,1)S(1)}, u32[]{:S(2)}, u32[]{:S(2)}) collective-permute-start(bf16[128,128]{1,0:T(8,128)(2,1)S(1)} %get-tuple-element.15), channel_id=1, source_target_pairs={{0,16},{16,0},{1,17},{17,1},{2,18},{18,2},{3,19},{19,3},{4,20},{20... | collective-permute-start | bytes 98312 | tf_op jit(solution)/shard_map/ppermute | solution.py:22

commit v2 on v1

v2 whole, which is shorter than its diff:
```python
import functools

import jax
import jax.numpy as jnp
from jax import lax
from jax.experimental import pallas as pl
from jax.experimental.pallas import tpu as pltpu
from jax.sharding import Mesh
from jax.sharding import PartitionSpec as P

AXES = ("y", "xl", "core", "xh", "z")
CHIPS = ("y", "xl")
COLS = ("xh", "z")
SWAP = [(0, 1), (1, 0)]
VMEM = pl.BlockSpec(memory_space=pltpu.VMEM)
SMEM = pl.BlockSpec(memory_space=pltpu.SMEM)
ANY = pl.BlockSpec(memory_space=pl.ANY)
DMA = pltpu.SemaphoreType.DMA
F32 = jnp.float32
BF16 = jnp.bfloat16


def swap(value):
    return lax.ppermute(value, "core", SWAP)


def exchange(value, axes):
    return lax.all_to_all(value, axes, 0, 0, tiled=True)


def copies_kernel(near, far, out):
    for which, half in enumerate((near, far)):
        out[:, which] = jnp.broadcast_to(half[...][None], (out.shape[0],) + half.shape)


def gathered_panels(mine, received, held, first, count):
    shape = (count, 2) + mine.shape

    def gather(near, far):
        copies = pl.pallas_call(
            copies_kernel,
            out_shape=jax.ShapeDtypeStruct(shape, near.dtype),
            in_specs=[VMEM] * 2,
            out_specs=VMEM,
            compiler_params=params(16),
        )(near, far)
        return exchange(copies, "y")

    def skip(near, far):
        return jnp.zeros(shape, near.dtype)

    panels = lax.cond(first, gather, skip, mine, received)
    panels, held = lax.optimization_barrier((panels, held))
    held = lax.ppermute(held, "core", [(0, 1)])
    panels = lax.cond(first, lambda near, far, done: done,
                      lambda near, far, done: gather(near, far), mine, held, panels)
    return panels, lax.ppermute(panels, "xl", SWAP)


def in_hbm(value):
    return pltpu.with_memory_space_constraint(value, pltpu.HBM)


def params(mib):
    return pltpu.CompilerParams(vmem_limit_bytes=mib * 1024 * 1024)


def dot(a, b, contract):
    return lax.dot_general(a, b, (contract, ((), ())), preferred_element_type=F32)


def source_onehot(order):
    size = order.shape[1]
    rows = lax.broadcasted_iota(jnp.int32, (size, size), 0)
    return (rows == order).astype(F32).astype(BF16)


def panel_kernel(ranges, core, order_in, rows_in, features, weight_in, cotangent,
                 mine, near_cot, pack, places, order, rows, weight, sem):
    size, half = mine.shape
    hid = 2 * half
    me = core[0]
    near = pl.ds(pl.multiple_of(me * half, half), half)
    far = pl.ds(pl.multiple_of((1 - me) * half, half), half)
    copies = [
        pltpu.make_async_copy(source, target, sem.at[index])
        for index, (source, target) in enumerate((
            (weight_in, weight),
            (features, pack.at[:size, hid:]),
            (order_in, order),
            (rows_in, rows),
            (cotangent.at[:, near], near_cot),
            (cotangent.at[:, far], pack.at[:size, half:hid]),
        ))
    ]
    for copy in copies:
        copy.start()
    for copy in copies:
        copy.wait()
    whole = dot(pack[:size, hid:], weight[...], ((1,), (0,))).astype(BF16)
    whole = dot(source_onehot(order[...]), whole, ((0,), (0,))).astype(BF16)
    first = me == 0
    left, right = whole[:, :half], whole[:, half:hid]
    mine[...] = jnp.where(first, left, right)
    pack[:size, :half] = jnp.where(first, right, left)
    extra = pack.shape[0] - size
    pack[size:, :] = jnp.zeros((extra, pack.shape[1]), BF16)
    numbers = (extra, size)
    pack[size:, :size] = jnp.broadcast_to(order[...].astype(F32), numbers).astype(BF16)
    ids = rows[:1]
    place = jnp.where(ids >= 0, lax.rem(ids, ranges), ranges)
    places[...] = place
    numbers = (extra, place.shape[1])
    place = jnp.broadcast_to(place.astype(F32), numbers).astype(BF16)
    pack[size:, size:size + place.shape[1]] = place


CHUNKS = 4


def forward_kernel(core_x, rows_own, rows_other, near_in, far_in, own, other_in, out,
                   near, far, other, total_own, total_other, sem):
    across, _, size, _ = near.shape
    ranges = out.shape[0]
    slots = own.shape[0] // (4 * across)
    me, x = core_x[0], core_x[1]
    part = other.shape[0] // CHUNKS
    arriving = [
        pltpu.make_async_copy(near_in, near, sem.at[CHUNKS]),
        pltpu.make_async_copy(far_in, far, sem.at[CHUNKS + 1]),
    ]
    for chunk in range(CHUNKS):
        tiles = pl.ds(chunk * part, part)
        arriving.append(
            pltpu.make_async_copy(other_in.at[tiles], other.at[tiles], sem.at[chunk]))
    for copy in arriving:
        copy.start()
    total_own[...] = jnp.zeros_like(total_own)
    total_other[...] = jnp.zeros_like(total_other)
    for copy in arriving:
        copy.wait()
    for panels, column in ((near, x), (far, 1 - x)):
        for y in range(across):
            for bit in range(2):
                panel = panels[y, bit ^ me]
                base = ((2 * y + column) * 2 + bit) * slots
                here = pl.ds(base, slots)
                ours = dot(own[here].reshape(slots * size, size), panel, ((1,), (0,)))
                theirs = dot(other[here].reshape(slots * size, size), panel, ((1,), (0,)))
                for slot in range(slots):
                    take = slice(slot * size, (slot + 1) * size)
                    total_own[rows_own[0, base + slot]] += ours[take]
                    total_other[rows_other[0, base + slot]] += theirs[take]
    for which, total in enumerate((total_own, total_other)):
        out[:, which] = total[:ranges].astype(BF16)


def middle_kernel(parts, near_cot, pack, hidden, grad):
    size, half = near_cot.shape
    scale = (2.0 / jnp.pi) ** 0.5
    for which in range(2):
        agg = jnp.sum(parts[:, which].astype(F32), axis=0)
        square = agg * agg
        slope = scale * (1.0 + 3.0 * 0.044715 * square)
        bend = jnp.tanh(scale * (agg + 0.044715 * (agg * square)))
        cdf = 0.5 * (1.0 + bend)
        hidden[which] = (agg * cdf).astype(BF16)
        upstream = near_cot[...] if which == 0 else pack[:size, half:2 * half]
        derivative = cdf + agg * (0.5 * (1.0 - bend * bend) * slope)
        turned = (upstream.astype(F32) * derivative).T.astype(BF16)
        grad[:, which] = jnp.broadcast_to(turned[None], (grad.shape[0],) + turned.shape)


def backward_kernel(core, rows_own, rows_other, grads, own, other_in, out, other, sem):
    chips = out.shape[0]
    ranges, _, _, size = grads.shape
    slots = own.shape[0] // (2 * chips)
    part = chips // CHUNKS
    me = core[0]
    arriving = []
    for chunk in range(CHUNKS):
        tiles = pl.ds(chunk * part * 2 * slots, part * 2 * slots)
        arriving.append(
            pltpu.make_async_copy(other_in.at[tiles], other.at[tiles], sem.at[chunk]))
        arriving[-1].start()
    for chunk in range(CHUNKS):
        arriving[chunk].wait()
        for group in range(2 * part * chunk, 2 * part * (chunk + 1)):
            lefts = []
            rights = []
            for which, (tiles, rows) in enumerate(((own, rows_own), (other, rows_other))):
                for slot in range(group * slots, (group + 1) * slots):
                    row = rows[0, slot]
                    block = grads[jnp.minimum(row, ranges - 1), which]
                    lefts.append(jnp.where(row < ranges, block, jnp.zeros_like(block)))
                here = slice(group * slots, (group + 1) * slots)
                rights.append(tiles[here].reshape(slots * size, size))
            left = jnp.concatenate(lefts, axis=1)
            right = jnp.concatenate(rights, axis=0)
            out[group // 2, (group % 2) ^ me] = dot(left, right, ((1,), (0,))).astype(BF16)


def weight_kernel(scale, parts, order, features, pack, turned, term):
    size = features.shape[0]
    hid = pack.shape[1] - features.shape[1]
    order_other = pack[size:, :size][:1].astype(F32).astype(jnp.int32)
    both = ((order[...], features[...]), (order_other, pack[:size, hid:]))
    total = 0.0
    for which, (source, values) in enumerate(both):
        panel_grad = jnp.sum(parts[:, which].astype(F32), axis=0).astype(BF16)
        placed = dot(panel_grad, source_onehot(source), ((1,), (1,))).astype(BF16)
        turned[which] = placed
        total = total + dot(placed, values, ((1,), (0,)))
    term[...] = (total * scale).T.astype(BF16)


def feature_kernel(core, mine, theirs, weight, out):
    half = mine.shape[0]
    me = core[0]
    near = weight[:, pl.ds(pl.multiple_of(me * half, half), half)]
    far = weight[:, pl.ds(pl.multiple_of((1 - me) * half, half), half)]
    total = dot(mine[...], near, ((0,), (1,))) + dot(theirs[...], far, ((0,), (1,)))
    out[...] = total.astype(BF16)


def per_device(features, node_order, weight, cotangent, tile_list, tile_values):
    tiles, size, _ = tile_values.shape
    in_width, hid = weight.shape
    half = hid // 2
    chips = lax.axis_size("y") * lax.axis_size("xl")
    ranges = lax.axis_size("xh") * lax.axis_size("z")
    nodes = 2 * chips * ranges * size
    core = lax.axis_index("core").astype(jnp.int32).reshape(1)
    first = core[0] == 0

    def joined(near, far):
        return jnp.where(
            first, jnp.concatenate([near, far], 1), jnp.concatenate([far, near], 1)
        )

    mine, near_cot, pack, rows_own = pl.pallas_call(
        functools.partial(panel_kernel, ranges),
        out_shape=[
            jax.ShapeDtypeStruct((size, half), BF16),
            jax.ShapeDtypeStruct((size, half), BF16),
            jax.ShapeDtypeStruct((size + 16, hid + in_width), BF16),
            jax.ShapeDtypeStruct((1, tiles), jnp.int32),
        ],
        in_specs=[SMEM] + [ANY] * 5,
        out_specs=[VMEM] * 4,
        scratch_shapes=[
            pltpu.VMEM((1, size), jnp.int32),
            pltpu.VMEM((2, tiles), jnp.int32),
            pltpu.VMEM((in_width, hid), BF16),
            DMA((6,)),
        ],
        compiler_params=params(16),
    )(core, *map(in_hbm, (node_order, tile_list.T, features, weight, cotangent)))
    held = pack[:size, :half]
    pack, later_tiles = lax.optimization_barrier((swap(pack), tile_values))
    tiles_other = swap(later_tiles)
    rows_other = pack[size:size + 1, size:size + tiles].astype(jnp.int32)
    across = lax.axis_size("y")
    near, far = gathered_panels(mine, pack[:size, :half], held, first, across)
    core_x = jnp.concatenate([core, lax.axis_index("xl").astype(jnp.int32).reshape(1)])

    partial = pl.pallas_call(
        forward_kernel,
        out_shape=jax.ShapeDtypeStruct((ranges, 2, size, half), BF16),
        in_specs=[SMEM, SMEM, SMEM, ANY, ANY, VMEM, ANY],
        out_specs=VMEM,
        scratch_shapes=[
            pltpu.VMEM((across, 2, size, half), BF16),
            pltpu.VMEM((across, 2, size, half), BF16),
            pltpu.VMEM((tiles, size, size), BF16),
            pltpu.VMEM((ranges + 1, size, half), F32),
            pltpu.VMEM((ranges + 1, size, half), F32),
            DMA((CHUNKS + 2,)),
        ],
        compiler_params=params(24),
    )(core_x, rows_own, rows_other, near, far, tile_values, tiles_other)
    parts = exchange(partial, COLS)
    hidden_pair, grad = pl.pallas_call(
        middle_kernel,
        out_shape=[
            jax.ShapeDtypeStruct((2, size, half), BF16),
            jax.ShapeDtypeStruct((ranges, 2, half, size), BF16),
        ],
        in_specs=[VMEM] * 3,
        out_specs=[VMEM] * 2,
        compiler_params=params(16),
    )(parts, near_cot, pack)
    grads = exchange(grad, COLS)
    contribution = pl.pallas_call(
        backward_kernel,
        out_shape=jax.ShapeDtypeStruct((chips, 2, half, size), BF16),
        in_specs=[SMEM, SMEM, SMEM, VMEM, VMEM, ANY],
        out_specs=VMEM,
        scratch_shapes=[
            pltpu.VMEM((tiles, size, size), BF16),
            DMA((CHUNKS,)),
        ],
        compiler_params=params(24),
    )(core, rows_own, rows_other, grads, tile_values, tiles_other)
    parts = exchange(contribution, CHIPS)
    turned, term = pl.pallas_call(
        functools.partial(weight_kernel, nodes ** -0.5),
        out_shape=[
            jax.ShapeDtypeStruct((2, half, size), BF16),
            jax.ShapeDtypeStruct((in_width, half), BF16),
        ],
        in_specs=[VMEM] * 4,
        out_specs=[VMEM] * 2,
        compiler_params=params(16),
    )(parts, node_order, features, pack)

    def summed(value):
        return jnp.sum(value.astype(F32), axis=0).astype(BF16)

    share = in_width // ranges
    term = summed(exchange(term.reshape(ranges, share, half), COLS))
    term = summed(exchange(jnp.broadcast_to(term[None], (chips, share, half)), CHIPS))
    term = exchange(jnp.broadcast_to(term[None], (ranges, share, half)), COLS)
    term = term.reshape(in_width, half)
    weight_grad = joined(term, swap(term)).astype(F32)

    late = swap(jnp.stack([hidden_pair[1], turned[1]]))
    hidden = joined(hidden_pair[0], late[0])
    x_grad = pl.pallas_call(
        feature_kernel,
        out_shape=jax.ShapeDtypeStruct((size, in_width), BF16),
        in_specs=[SMEM, VMEM, VMEM, VMEM],
        out_specs=VMEM,
        compiler_params=params(16),
    )(core, turned[0], late[1], weight)
    return (hidden, x_grad, weight_grad)


def solution(mesh):
    blk, col = mesh.devices.shape
    fine = Mesh(mesh.devices.reshape(blk // 4, 2, 2, 2, col // 2), AXES)
    rows = P(AXES)
    return jax.shard_map(
        per_device,
        mesh=fine,
        in_specs=(rows, rows, P(), rows, rows, rows),
        out_specs=(rows, rows, P()),
        check_vma=False,
    )
```

time: 223 us -> 188 us (0.84)
  starting transfers between devices: 70 us -> 25.2 us
  blocking collectives: 63.2 us -> 103 us
  waiting for transfers between devices: 63.7 us -> 41.9 us
  local copies, waits for them, and re-layouts: 6.61 us -> 2.36 us
  Pallas kernels: 16.3 us -> 12.6 us
    all_to_all x4 -> x2, waiting for transfers between devices: 59.1 us -> 16 us  [exchange(): return lax.all_to_all(value, axes, 0, 0, tiled=True)]
    all_to_all x3 -> x5, blocking collectives: 63.2 us -> 103 us  [exchange(): return lax.all_to_all(value, axes, 0, 0, tiled=True)]
    ppermute x9 -> x4, starting transfers between devices: 39.5 us -> 14.9 us  [swap(): return lax.ppermute(value, 'core', SWAP)]
    ppermute x0 -> x2, waiting for transfers between devices: none -> 24.6 us  [the longest x1 16.4 us: gathered_panels(): held = lax.ppermute(held, 'core', [(0, 1)])]
    all_to_all x4 -> x2, starting transfers between devices: 30.5 us -> 7.15 us  [exchange(): return lax.all_to_all(value, axes, 0, 0, tiled=True)]
    unnamed x22 -> x8, local copies, waits for them, and re-layouts: 4.61 us -> 0.02 us
    ppermute x9 -> x4, waiting for transfers between devices: 4.56 us -> 1.19 us  [swap(): return lax.ppermute(value, 'core', SWAP)]
    ppermute x0 -> x2, starting transfers between devices: none -> 3.19 us  [the longest x1 1.91 us: gathered_panels(): return (panels, lax.ppermute(panels, 'xl', SWAP))]
  transfers between devices with their start and end apart: 13 -> 8, of which waited for: 9 -> 5; matrix products, arithmetic and copies ran while one was open for 1% -> 1% of each run, Pallas kernels for 1% -> 1%
where the time goes in v2:
time: 188 us
  blocking collectives  103 us (55%)
  waiting for transfers between devices  41.9 us (22%)
  starting transfers between devices  25.2 us (13%)
  Pallas kernels  12.6 us (7%)
  local copies, waits for them, and re-layouts  2.36 us (1%)
    all_to_all x5, blocking collectives, exchange(): return lax.all_to_all(value, axes, 0, 0, tiled=True)  103 us
    ppermute x1, waiting for transfers between devices, gathered_panels(): held = lax.ppermute(held, 'core', [(0, 1)])  16.4 us
    all_to_all x2, waiting for transfers between devices, exchange(): return lax.all_to_all(value, axes, 0, 0, tiled=True)  16 us
    ppermute x4, starting transfers between devices, swap(): return lax.ppermute(value, 'core', SWAP)  14.9 us
    ppermute x1, waiting for transfers between devices, gathered_panels(): return (panels, lax.ppermute(panels, 'xl', SWAP))  8.23 us
    all_to_all x2, starting transfers between devices, exchange(): return lax.all_to_all(value, axes, 0, 0, tiled=True)  7.15 us
    pallas_call x1, Pallas kernels, per_device(): pl.pallas_call(forward_kernel, out_shape=jax.ShapeDtypeStruct((ranges, 2,...  4.76 us
    pallas_call x1, Pallas kernels, per_device(): pl.pallas_call(backward_kernel, out_shape=jax.ShapeDtypeStruct((chips, 2,...  4.2 us
  transfers between devices with their start and end apart: 8, of which 5 were waited for; matrix products, arithmetic and copies ran while one was open for 1% of the time, Pallas kernels for 1%

profile of v2, /device:TPU:1, one launch (start us, length us, event | category | flops | bytes accessed | tf_op | source)
XLA Modules:
  0.0 187.5 jit_solution(9225338650670654233)
XLA Ops:
  0.6 0.0 copy-start
  0.6 1.6 shard_map.85
  2.3 8.8 %collective-permute-start = (bf16[144,1024]{1,0:T(8,128)(2,1)S(1)}, bf16[144,1024]{1,0:T(8,128)(2,1)S(1)}, u32[]{:S(2)}, u32[]{:S(2)}) collective-permute-start(bf16[144,1024]{1,0:T(8,128)(2,1)S(1)} %get-tuple-element.36), channel_id=1, source_target_pairs={{0,16},{16,0},{1,17},{17,1},{2,18},{18,2},{3,19},{19,3},{4,20},{20... | collective-permute-start | bytes 884744 | tf_op jit(solution)/shard_map/ppermute | solution.py:24
  11.1 1.2 collective-permute-done.pack
  12.3 2.3 %collective-permute-start.3 = (bf16[96,128,128]{2,1,0:T(8,128)(2,1)}, bf16[96,128,128]{2,1,0:T(8,128)(2,1)}, u32[]{:S(2)}, u32[]{:S(2)}) collective-permute-start(bf16[96,128,128]{2,1,0:T(8,128)(2,1)} %own.3), channel_id=1, source_target_pairs={{0,16},{16,0},{1,17},{17,1},{2,18},{18,2},{3,19},{19,3},{4,20},{20... | collective-permute-start | bytes 9437192 | tf_op jit(solution)/shard_map/ppermute | solution.py:24
  14.6 0.9 conditional.2
  14.6 0.9 broadcast.4
  15.5 1.3 collective-permute-start.1
  16.8 16.4 %collective-permute-done.1 = bf16[128,128]{1,0:T(8,128)(2,1)S(1)} collective-permute-done((bf16[128,128]{1,0:T(8,128)(2,1)S(1)}, bf16[128,128]{1,0:T(8,128)(2,1)S(1)}, u32[]{:S(2)}, u32[]{:S(2)}) %collective-permute-start.1) | collective-permute-done | bytes 32800 | tf_op jit(solution)/shard_map/ppermute | solution.py:54
  33.2 15.3 %conditional.3 = (bf16[8,2,128,128]{3,2,1,0:T(8,128)(2,1)}) conditional(s32[]{:T(128)} %convert_element_type.7, (bf16[128,128]{1,0:T(8,128)(2,1)S(1)}, bf16[128,128]{1,0:T(8,128)(2,1)S(1)}) %tuple.26, bf16[8,2,128,128]{3,2,1,0:T(8,128)(2,1)} %get-tuple-element.53), branch_computations={%region_2.0_spmd, %region_3.0_spmd} | conditional | bytes 1048584 | solution.py:55
  33.2 0.1 branch_0_fun.1
  33.3 15.2 %all_to_all.39 = bf16[8,2,128,128]{3,2,1,0:T(8,128)(2,1)} all-to-all(bf16[8,2,128,128]{3,2,1,0:T(8,128)(2,1)S(1)} %branch_0_fun.1), channel_id=1, replica_groups=mesh['y'=8,'xl'=2,'core'=2,'xh'=2,'z'=8] {'y'}, dimensions={0} | all-to-all | bytes 1048576 | tf_op jit(solution)/shard_map/cond/branch_0_fun/all_to_all | solution.py:28
  48.5 1.9 %collective-permute-start.2 = (bf16[8,2,128,128]{3,2,1,0:T(8,128)(2,1)}, bf16[8,2,128,128]{3,2,1,0:T(8,128)(2,1)}, u32[]{:S(2)}, u32[]{:S(2)}) collective-permute-start(bf16[8,2,128,128]{3,2,1,0:T(8,128)(2,1)} %get-tuple-element.54.near_in), channel_id=1, source_target_pairs={{0,32},{32,0},{1,33},{33,1},{2,34},{34,2},{3,35},{35,3},{4,36},{36... | collective-permute-start | bytes 1572872 | tf_op jit(solution)/shard_map/ppermute | solution.py:57
  50.4 0.1 pad_add_fusion.core_x
  50.5 8.2 %collective-permute-done.2.far_in = bf16[8,2,128,128]{3,2,1,0:T(8,128)(2,1)} collective-permute-done((bf16[8,2,128,128]{3,2,1,0:T(8,128)(2,1)}, bf16[8,2,128,128]{3,2,1,0:T(8,128)(2,1)}, u32[]{:S(2)}, u32[]{:S(2)}) %collective-permute-start.2) | collective-permute-done | bytes 524320 | tf_op jit(solution)/shard_map/ppermute | solution.py:57
  58.7 0.0 collective-permute-done.3.other_in
  58.7 0.0 copy-done
  58.7 4.8 %shard_map.86 = bf16[16,2,128,128]{3,2,1,0:T(8,128)(2,1)S(1)} custom-call(s32[2]{0:T(128)S(1)} %pad_add_fusion.core_x, s32[1,96]{1,0:T(1,128)S(1)} %get-tuple-element.35.rows_own, s32[1,96]{1,0:T(1,128)S(1)} %slice_convert_fusion.rows_other, bf16[8,2,128,128]{3,2,1,0:T(8,128)(2,1)} %get-tuple-element.54.near_in, ...), custom_call_target="tpu_custom_call" | custom-call | tf_op jit(solution)/shard_map/pallas_call | solution.py:267
  63.5 28.5 %all_to_all.40.parts = bf16[16,2,128,128]{3,2,1,0:T(8,128)(2,1)S(1)} all-to-all(bf16[16,2,128,128]{3,2,1,0:T(8,128)(2,1)S(1)} %shard_map.86), channel_id=1, replica_groups=mesh['y'=8,'xl'=2,'core'=2,'xh'=2,'z'=8] {'xh','z'}, dimensions={0} | all-to-all | bytes 2097152 | tf_op jit(solution)/shard_map/all_to_all | solution.py:28
  92.0 0.4 shard_map.87
  92.4 23.0 %all_to_all.41.grads = bf16[16,2,128,128]{3,2,1,0:T(8,128)(2,1)S(1)} all-to-all(bf16[16,2,128,128]{3,2,1,0:T(8,128)(2,1)S(1)} %get-tuple-element.44), channel_id=1, replica_groups=mesh['y'=8,'xl'=2,'core'=2,'xh'=2,'z'=8] {'xh','z'}, dimensions={0} | all-to-all | bytes 2097152 | tf_op jit(solution)/shard_map/all_to_all | solution.py:28
  115.4 0.0 copy-start.2
  115.4 0.0 copy-start.3
  115.4 4.2 %shard_map.88 = bf16[16,2,128,128]{3,2,1,0:T(8,128)(2,1)S(1)} custom-call(s32[1]{0:T(128)} %bitcast.core, s32[1,96]{1,0:T(1,128)S(1)} %get-tuple-element.35.rows_own, s32[1,96]{1,0:T(1,128)S(1)} %slice_convert_fusion.rows_other, bf16[16,2,128,128]{3,2,1,0:T(8,128)(2,1)S(1)} %all_to_all.41.grads, bf16[96,128,128]{2,1,0:T(8,128)(2,1)S(1)} %copy-done, ...), custom_call_target="tpu_custom_call" | custom-call | tf_op jit(solution)/shard_map/pallas_call | solution.py:294
  119.6 0.0 copy-start.1
  119.6 22.8 %all_to_all.42.parts = bf16[16,2,128,128]{3,2,1,0:T(8,128)(2,1)S(1)} all-to-all(bf16[16,2,128,128]{3,2,1,0:T(8,128)(2,1)S(1)} %shard_map.88), channel_id=1, replica_groups=mesh['y'=8,'xl'=2,'core'=2,'xh'=2,'z'=8] {'y','xl'}, dimensions={0} | all-to-all | bytes 2097152 | tf_op jit(solution)/shard_map/all_to_all | solution.py:28
  142.4 0.0 copy-done.2
  142.4 0.0 copy-done.3
  142.4 0.6 shard_map.89
  143.0 13.3 %all_to_all.43 = bf16[16,48,128]{2,1,0:T(8,128)(2,1)S(1)} all-to-all(bf16[16,48,128]{2,1,0:T(8,128)(2,1)S(1)} %bitcast.13), channel_id=1, replica_groups=mesh['y'=8,'xl'=2,'core'=2,'xh'=2,'z'=8] {'xh','z'}, dimensions={0} | all-to-all | bytes 393216 | tf_op jit(solution)/shard_map/all_to_all | solution.py:28
  156.3 0.7 broadcast_in_dim.4
  157.0 3.5 %all-to-all-start.6 = ((bf16[16,48,128]{2,1,0:T(8,128)(2,1)}), bf16[16,48,128]{2,1,0:T(8,128)(2,1)S(1)}, u32[]{:S(2)}, u32[]{:S(2)}) async-start(bf16[16,48,128]{2,1,0:T(8,128)(2,1)} %broadcast_in_dim.4), calls=%async_computation.6 | async-start | bytes 393216 | tf_op jit(solution)/shard_map/all_to_all | solution.py:28
  160.6 9.0 %all-to-all-done.6 = bf16[16,48,128]{2,1,0:T(8,128)(2,1)S(1)} async-done(((bf16[16,48,128]{2,1,0:T(8,128)(2,1)}), bf16[16,48,128]{2,1,0:T(8,128)(2,1)S(1)}, u32[]{:S(2)}, u32[]{:S(2)}) %all-to-all-start.6) | async-done | bytes 196640 | tf_op jit(solution)/shard_map/all_to_all | solution.py:28
  169.6 0.7 broadcast_in_dim.5
  170.3 3.6 %all-to-all-start.7 = ((bf16[16,48,128]{2,1,0:T(8,128)(2,1)}), bf16[16,48,128]{2,1,0:T(8,128)(2,1)S(1)}, u32[]{:S(2)}, u32[]{:S(2)}) async-start(bf16[16,48,128]{2,1,0:T(8,128)(2,1)} %broadcast_in_dim.5), calls=%async_computation.7 | async-start | bytes 393216 | tf_op jit(solution)/shard_map/all_to_all | solution.py:28
  174.0 1.9 %collective-permute-start.4 = (bf16[2,128,128]{2,1,0:T(8,128)(2,1)S(1)}, bf16[2,128,128]{2,1,0:T(8,128)(2,1)S(1)}, u32[]{:S(2)}, u32[]{:S(2)}) collective-permute-start(bf16[2,128,128]{2,1,0:T(8,128)(2,1)S(1)} %pad_maximum_fusion), channel_id=1, source_target_pairs={{0,16},{16,0},{1,17},{17,1},{2,18},{18,2},{3,19},{19,3},{4,20},{20... | collective-permute-start | bytes 196616 | tf_op jit(solution)/shard_map/ppermute | solution.py:24
  175.9 7.0 %all-to-all-done.7 = bf16[16,48,128]{2,1,0:T(8,128)(2,1)S(1)} async-done(((bf16[16,48,128]{2,1,0:T(8,128)(2,1)}), bf16[16,48,128]{2,1,0:T(8,128)(2,1)S(1)}, u32[]{:S(2)}, u32[]{:S(2)}) %all-to-all-start.7) | async-done | bytes 196640 | tf_op jit(solution)/shard_map/all_to_all | solution.py:28
  182.9 1.9 %collective-permute-start.5 = (bf16[768,128]{1,0:T(8,128)(2,1)S(1)}, bf16[768,128]{1,0:T(8,128)(2,1)S(1)}, u32[]{:S(2)}, u32[]{:S(2)}) collective-permute-start(bf16[768,128]{1,0:T(8,128)(2,1)S(1)} %bitcast.14), channel_id=1, source_target_pairs={{0,16},{16,0},{1,17},{17,1},{2,18},{18,2},{3,19},{19,3},{4,20},{20... | collective-permute-start | bytes 589832 | tf_op jit(solution)/shard_map/ppermute | solution.py:24
  184.9 0.0 collective-permute-done.4
  184.9 0.0 copy-done.1
  184.9 1.0 shard_map.90
  185.9 0.6 maximum_select_fusion.1
  186.5 0.0 collective-permute-done.5
  186.5 1.0 fusion
  (8 shorter events, 0.1 us)
Async XLA Ops:
  0.6 58.1 %copy-start = (bf16[96,128,128]{2,1,0:T(8,128)(2,1)S(1)}, bf16[96,128,128]{2,1,0:T(8,128)(2,1)}, u32[]{:S(2)}) copy-start(bf16[96,128,128]{2,1,0:T(8,128)(2,1)} %own.3) | copy-start | bytes 9437188
  2.3 10.0 %collective-permute-start = (bf16[144,1024]{1,0:T(8,128)(2,1)S(1)}, bf16[144,1024]{1,0:T(8,128)(2,1)S(1)}, u32[]{:S(2)}, u32[]{:S(2)}) collective-permute-start(bf16[144,1024]{1,0:T(8,128)(2,1)S(1)} %get-tuple-element.36), channel_id=1, source_target_pairs={{0,16},{16,0},{1,17},{17,1},{2,18},{18,2},{3,19},{19,3},{4,20},{20... | collective-permute-start | bytes 884744 | tf_op jit(solution)/shard_map/ppermute | solution.py:24
  12.3 46.4 %collective-permute-start.3 = (bf16[96,128,128]{2,1,0:T(8,128)(2,1)}, bf16[96,128,128]{2,1,0:T(8,128)(2,1)}, u32[]{:S(2)}, u32[]{:S(2)}) collective-permute-start(bf16[96,128,128]{2,1,0:T(8,128)(2,1)} %own.3), channel_id=1, source_target_pairs={{0,16},{16,0},{1,17},{17,1},{2,18},{18,2},{3,19},{19,3},{4,20},{20... | collective-permute-start | bytes 9437192 | tf_op jit(solution)/shard_map/ppermute | solution.py:24
  15.5 17.7 %collective-permute-start.1 = (bf16[128,128]{1,0:T(8,128)(2,1)S(1)}, bf16[128,128]{1,0:T(8,128)(2,1)S(1)}, u32[]{:S(2)}, u32[]{:S(2)}) collective-permute-start(bf16[128,128]{1,0:T(8,128)(2,1)S(1)} %slice.29), channel_id=1, source_target_pairs={{0,16},{1,17},{2,18},{3,19},{4,20},{5,21},{6,22},{7,23},{8,24},{9,... | collective-permute-start | bytes 98312 | tf_op jit(solution)/shard_map/ppermute | solution.py:54
  48.5 10.2 %collective-permute-start.2 = (bf16[8,2,128,128]{3,2,1,0:T(8,128)(2,1)}, bf16[8,2,128,128]{3,2,1,0:T(8,128)(2,1)}, u32[]{:S(2)}, u32[]{:S(2)}) collective-permute-start(bf16[8,2,128,128]{3,2,1,0:T(8,128)(2,1)} %get-tuple-element.54.near_in), channel_id=1, source_target_pairs={{0,32},{32,0},{1,33},{33,1},{2,34},{34,2},{3,35},{35,3},{4,36},{36... | collective-permute-start | bytes 1572872 | tf_op jit(solution)/shard_map/ppermute | solution.py:57
  115.4 27.0 %copy-start.2 = (bf16[128,768]{1,0:T(8,128)(2,1)S(1)}, bf16[128,768]{1,0:T(8,128)(2,1)}, u32[]{:S(2)}) copy-start(bf16[128,768]{1,0:T(8,128)(2,1)} %features.3) | copy-start | bytes 589828
  115.4 27.0 %copy-start.3 = (s32[1,128]{1,0:T(1,128)S(1)}, s32[1,128]{1,0:T(1,128)}, u32[]{:S(2)}) copy-start(s32[1,128]{1,0:T(1,128)} %order.1) | copy-start | bytes 1540
  119.6 65.3 %copy-start.1 = (bf16[768,256]{1,0:T(8,128)(2,1)S(1)}, bf16[768,256]{1,0:T(8,128)(2,1)}, u32[]{:S(2)}) copy-start(bf16[768,256]{1,0:T(8,128)(2,1)} %weight.1) | copy-start | bytes 1179652
  157.0 12.6 %all-to-all-start.6 = ((bf16[16,48,128]{2,1,0:T(8,128)(2,1)}), bf16[16,48,128]{2,1,0:T(8,128)(2,1)S(1)}, u32[]{:S(2)}, u32[]{:S(2)}) async-start(bf16[16,48,128]{2,1,0:T(8,128)(2,1)} %broadcast_in_dim.4), calls=%async_computation.6 | async-start | bytes 393216 | tf_op jit(solution)/shard_map/all_to_all | solution.py:28
  170.3 12.6 %all-to-all-start.7 = ((bf16[16,48,128]{2,1,0:T(8,128)(2,1)}), bf16[16,48,128]{2,1,0:T(8,128)(2,1)S(1)}, u32[]{:S(2)}, u32[]{:S(2)}) async-start(bf16[16,48,128]{2,1,0:T(8,128)(2,1)} %broadcast_in_dim.5), calls=%async_computation.7 | async-start | bytes 393216 | tf_op jit(solution)/shard_map/all_to_all | solution.py:28
  174.0 10.9 %collective-permute-start.4 = (bf16[2,128,128]{2,1,0:T(8,128)(2,1)S(1)}, bf16[2,128,128]{2,1,0:T(8,128)(2,1)S(1)}, u32[]{:S(2)}, u32[]{:S(2)}) collective-permute-start(bf16[2,128,128]{2,1,0:T(8,128)(2,1)S(1)} %pad_maximum_fusion), channel_id=1, source_target_pairs={{0,16},{16,0},{1,17},{17,1},{2,18},{18,2},{3,19},{19,3},{4,20},{20... | collective-permute-start | bytes 196616 | tf_op jit(solution)/shard_map/ppermute | solution.py:24
  182.9 3.6 %collective-permute-start.5 = (bf16[768,128]{1,0:T(8,128)(2,1)S(1)}, bf16[768,128]{1,0:T(8,128)(2,1)S(1)}, u32[]{:S(2)}, u32[]{:S(2)}) collective-permute-start(bf16[768,128]{1,0:T(8,128)(2,1)S(1)} %bitcast.14), channel_id=1, source_target_pairs={{0,16},{16,0},{1,17},{17,1},{2,18},{18,2},{3,19},{19,3},{4,20},{20... | collective-permute-start | bytes 589832 | tf_op jit(solution)/shard_map/ppermute | solution.py:24

commit v3 on v2

--- a/solution.py
+++ b/solution.py
@@ -18,6 +18,7 @@
 DMA = pltpu.SemaphoreType.DMA
 F32 = jnp.float32
 BF16 = jnp.bfloat16
+SLOTS = 3
 
 
 def swap(value):
@@ -115,44 +116,69 @@
     pack[size:, size:size + place.shape[1]] = place
 
 
-CHUNKS = 4
-
-
-def forward_kernel(core_x, rows_own, rows_other, near_in, far_in, own, other_in, out,
-                   near, far, other, total_own, total_other, sem):
-    across, _, size, _ = near.shape
+def multiply(y, column, me, rows_own, rows_other, panels, own, other, total):
+    size = own.shape[1]
+    for bit in range(2):
+        panel = panels[y, bit ^ me]
+        base = ((2 * y + column) * 2 + bit) * SLOTS
+        here = pl.ds(base, SLOTS)
+        ours = dot(own[here].reshape(SLOTS * size, size), panel, ((1,), (0,)))
+        theirs = dot(other[here].reshape(SLOTS * size, size), panel, ((1,), (0,)))
+        for slot in range(SLOTS):
+            take = slice(slot * size, (slot + 1) * size)
+            total[0, rows_own[0, base + slot]] += ours[take]
+            total[1, rows_other[0, base + slot]] += theirs[take]
+
+
+def near_kernel(core_x, rows_own, rows_other, panels_in, own_in, other_in,
+                total, own, other, panels, sem):
+    across = panels.shape[0]
+    me, x = core_x[0], core_x[1]
+    groups = 2 * SLOTS
+    sooner = []
+    later = []
+    for y in range(across):
+        sooner.append(pltpu.make_async_copy(panels_in.at[y], panels.at[y], sem.at[5 * y]))
+        for turn, copies in enumerate((sooner, later)):
+            column = x if turn == 0 else 1 - x
+            tiles = pl.ds((2 * y + column) * groups, groups)
+            for which, (source, target) in enumerate(((own_in, own), (other_in, other))):
+                copies.append(pltpu.make_async_copy(
+                    source.at[tiles], target.at[tiles], sem.at[5 * y + 1 + 2 * turn + which]))
+    for copy in sooner + later:
+        copy.start()
+    total[...] = jnp.zeros_like(total)
+    for y in range(across):
+        for copy in sooner[3 * y:3 * y + 3]:
+            copy.wait()
+        multiply(y, x, me, rows_own, rows_other, panels, own, other, total)
+    for copy in later:
+        copy.wait()
+
+
+def far_kernel(core_x, rows_own, rows_other, panels, own, other, before, out, total):
     ranges = out.shape[0]
-    slots = own.shape[0] // (4 * across)
     me, x = core_x[0], core_x[1]
-    part = other.shape[0] // CHUNKS
-    arriving = [
-        pltpu.make_async_copy(near_in, near, sem.at[CHUNKS]),
-        pltpu.make_async_copy(far_in, far, sem.at[CHUNKS + 1]),
-    ]
-    for chunk in range(CHUNKS):
-        tiles = pl.ds(chunk * part, part)
-        arriving.append(
-            pltpu.make_async_copy(other_in.at[tiles], other.at[tiles], sem.at[chunk]))
-    for copy in arriving:
-        copy.start()
-    total_own[...] = jnp.zeros_like(total_own)
-    total_other[...] = jnp.zeros_like(total_other)
-    for copy in arriving:
-        copy.wait()
-    for panels, column in ((near, x), (far, 1 - x)):
-        for y in range(across):
-            for bit in range(2):
-                panel = panels[y, bit ^ me]
-                base = ((2 * y + column) * 2 + bit) * slots
-                here = pl.ds(base, slots)
-                ours = dot(own[here].reshape(slots * size, size), panel, ((1,), (0,)))
-                theirs = dot(other[here].reshape(slots * size, size), panel, ((1,), (0,)))
-                for slot in range(slots):
-                    take = slice(slot * size, (slot + 1) * size)
-                    total_own[rows_own[0, base + slot]] += ours[take]
-                    total_other[rows_other[0, base + slot]] += theirs[take]
-    for which, total in enumerate((total_own, total_other)):
-        out[:, which] = total[:ranges].astype(BF16)
+    total[...] = jnp.zeros_like(total)
+    for y in range(panels.shape[0]):
+        multiply(y, 1 - x, me, rows_own, rows_other, panels, own, other, total)
+    for which in range(2):
+        out[:, which] = (before[which, :ranges] + total[which, :ranges]).astype(BF16)
+
+
+def spread_kernel(parts, out):
+    total = jnp.sum(parts[...].astype(F32), axis=0).astype(BF16)
+    out[...] = jnp.broadcast_to(total[None], out.shape)
+
+
+def spread(parts, count):
+    return pl.pallas_call(
+        spread_kernel,
+        out_shape=jax.ShapeDtypeStruct((count,) + parts.shape[1:], parts.dtype),
+        in_specs=[VMEM],
+        out_specs=VMEM,
+        compiler_params=params(16),
+    )(parts)
 
 
 def middle_kernel(parts, near_cot, pack, hidden, grad):
@@ -171,33 +197,24 @@
         grad[:, which] = jnp.broadcast_to(turned[None], (grad.shape[0],) + turned.shape)
 
 
-def backward_kernel(core, rows_own, rows_other, grads, own, other_in, out, other, sem):
+def backward_kernel(core, rows_own, rows_other, grads, own, other, out):
     chips = out.shape[0]
     ranges, _, _, size = grads.shape
     slots = own.shape[0] // (2 * chips)
-    part = chips // CHUNKS
     me = core[0]
-    arriving = []
-    for chunk in range(CHUNKS):
-        tiles = pl.ds(chunk * part * 2 * slots, part * 2 * slots)
-        arriving.append(
-            pltpu.make_async_copy(other_in.at[tiles], other.at[tiles], sem.at[chunk]))
-        arriving[-1].start()
-    for chunk in range(CHUNKS):
-        arriving[chunk].wait()
-        for group in range(2 * part * chunk, 2 * part * (chunk + 1)):
-            lefts = []
-            rights = []
-            for which, (tiles, rows) in enumerate(((own, rows_own), (other, rows_other))):
-                for slot in range(group * slots, (group + 1) * slots):
-                    row = rows[0, slot]
-                    block = grads[jnp.minimum(row, ranges - 1), which]
-                    lefts.append(jnp.where(row < ranges, block, jnp.zeros_like(block)))
-                here = slice(group * slots, (group + 1) * slots)
-                rights.append(tiles[here].reshape(slots * size, size))
-            left = jnp.concatenate(lefts, axis=1)
-            right = jnp.concatenate(rights, axis=0)
-            out[group // 2, (group % 2) ^ me] = dot(left, right, ((1,), (0,))).astype(BF16)
+    for group in range(2 * chips):
+        lefts = []
+        rights = []
+        here = slice(group * slots, (group + 1) * slots)
+        for which, (tiles, rows) in enumerate(((own, rows_own), (other, rows_other))):
+            for slot in range(group * slots, (group + 1) * slots):
+                row = rows[0, slot]
+                block = grads[jnp.minimum(row, ranges - 1), which]
+                lefts.append(jnp.where(row < ranges, block, jnp.zeros_like(block)))
+            rights.append(tiles[here].reshape(slots * size, size))
+        left = jnp.concatenate(lefts, axis=1)
+        right = jnp.concatenate(rights, axis=0)
+        out[group // 2, (group % 2) ^ me] = dot(left, right, ((1,), (0,))).astype(BF16)
 
 
 def weight_kernel(scale, parts, order, features, pack, turned, term):
@@ -264,21 +281,34 @@
     near, far = gathered_panels(mine, pack[:size, :half], held, first, across)
     core_x = jnp.concatenate([core, lax.axis_index("xl").astype(jnp.int32).reshape(1)])
 
+    total_shape = (2, ranges + 1, size, half)
+    half_cost = pl.CostEstimate(
+        flops=2 * tiles * size * size * half,
+        bytes_accessed=tiles * size * size * 4,
+        transcendentals=0,
+    )
+    partial, tiles_own, tiles_other = pl.pallas_call(
+        near_kernel,
+        out_shape=[
+            jax.ShapeDtypeStruct(total_shape, F32),
+            jax.ShapeDtypeStruct(tile_values.shape, BF16),
+            jax.ShapeDtypeStruct(tile_values.shape, BF16),
+        ],
+        in_specs=[SMEM, SMEM, SMEM, ANY, ANY, ANY],
+        out_specs=[VMEM] * 3,
+        scratch_shapes=[pltpu.VMEM((across, 2, size, half), BF16), DMA((5 * across,))],
+        compiler_params=params(24),
+        cost_estimate=half_cost,
+    )(core_x, rows_own, rows_other, *map(in_hbm, (near, tile_values, tiles_other)))
     partial = pl.pallas_call(
-        forward_kernel,
+        far_kernel,
         out_shape=jax.ShapeDtypeStruct((ranges, 2, size, half), BF16),
-        in_specs=[SMEM, SMEM, SMEM, ANY, ANY, VMEM, ANY],
+        in_specs=[SMEM, SMEM, SMEM] + [VMEM] * 4,
         out_specs=VMEM,
-        scratch_shapes=[
-            pltpu.VMEM((across, 2, size, half), BF16),
-            pltpu.VMEM((across, 2, size, half), BF16),
-            pltpu.VMEM((tiles, size, size), BF16),
-            pltpu.VMEM((ranges + 1, size, half), F32),
-            pltpu.VMEM((ranges + 1, size, half), F32),
-            DMA((CHUNKS + 2,)),
-        ],
+        scratch_shapes=[pltpu.VMEM(total_shape, F32)],
         compiler_params=params(24),
-    )(core_x, rows_own, rows_other, near, far, tile_values, tiles_other)
+        cost_estimate=half_cost,
+    )(core_x, rows_own, rows_other, far, tiles_own, tiles_other, partial)
     parts = exchange(partial, COLS)
     hidden_pair, grad = pl.pallas_call(
         middle_kernel,
@@ -294,14 +324,10 @@
     contribution = pl.pallas_call(
         backward_kernel,
         out_shape=jax.ShapeDtypeStruct((chips, 2, half, size), BF16),
-        in_specs=[SMEM, SMEM, SMEM, VMEM, VMEM, ANY],
+        in_specs=[SMEM, SMEM, SMEM, VMEM, VMEM, VMEM],
         out_specs=VMEM,
-        scratch_shapes=[
-            pltpu.VMEM((tiles, size, size), BF16),
-            DMA((CHUNKS,)),
-        ],
         compiler_params=params(24),
-    )(core, rows_own, rows_other, grads, tile_values, tiles_other)
+    )(core, rows_own, rows_other, grads, tiles_own, tiles_other)
     parts = exchange(contribution, CHIPS)
     turned, term = pl.pallas_call(
         functools.partial(weight_kernel, nodes ** -0.5),
@@ -314,13 +340,10 @@
         compiler_params=params(16),
     )(parts, node_order, features, pack)
 
-    def summed(value):
-        return jnp.sum(value.astype(F32), axis=0).astype(BF16)
-
     share = in_width // ranges
-    term = summed(exchange(term.reshape(ranges, share, half), COLS))
-    term = summed(exchange(jnp.broadcast_to(term[None], (chips, share, half)), CHIPS))
-    term = exchange(jnp.broadcast_to(term[None], (ranges, share, half)), COLS)
+    term = exchange(term.reshape(ranges, share, half), COLS)
+    term = exchange(spread(term, chips), CHIPS)
+    term = exchange(spread(term, ranges), COLS)
     term = term.reshape(in_width, half)
     weight_grad = joined(term, swap(term)).astype(F32)
 

time: 188 us -> 186 us (0.989)
  waiting for transfers between devices: 41.9 us -> 37.2 us
  blocking collectives: 103 us -> 106 us
  local copies, waits for them, and re-layouts: 2.36 us -> 0.14 us
    ppermute x1, waiting for transfers between devices: 8.23 us -> 3.5 us  [gathered_panels(): return (panels, lax.ppermute(panels, 'xl', SWAP))]
    all_to_all x5, blocking collectives: 103 us -> 106 us  [exchange(): return lax.all_to_all(value, axes, 0, 0, tiled=True)]
    pallas_call x1 -> x4, Pallas kernels: 4.76 us -> 7.44 us  [the longest x1 4.08 us: per_device(): pl.pallas_call(near_kernel, out_shape=[jax.ShapeDtypeStruct(total_shape,...]
  transfers between devices with their start and end apart: 8 -> 8, of which waited for: 5 -> 5; matrix products, arithmetic and copies ran while one was open for 1% -> 0% of each run, Pallas kernels for 1% -> 3%
where the time goes in v3:
time: 186 us; the launch traced here: 185 us
  blocking collectives  106 us (57%)
  waiting for transfers between devices  37.2 us (20%)
  starting transfers between devices  25.8 us (14%)
  Pallas kernels  13.4 us (7%)
    all_to_all x5, blocking collectives, exchange(): return lax.all_to_all(value, axes, 0, 0, tiled=True)  106 us
    ppermute x1, waiting for transfers between devices, gathered_panels(): held = lax.ppermute(held, 'core', [(0, 1)])  16.5 us
    all_to_all x2, waiting for transfers between devices, exchange(): return lax.all_to_all(value, axes, 0, 0, tiled=True)  16 us
    ppermute x4, starting transfers between devices, swap(): return lax.ppermute(value, 'core', SWAP)  14.9 us
    all_to_all x2, starting transfers between devices, exchange(): return lax.all_to_all(value, axes, 0, 0, tiled=True)  7.44 us
    pallas_call x1, Pallas kernels, per_device(): pl.pallas_call(near_kernel, out_shape=[jax.ShapeDtypeStruct(total_shape,...  4.08 us
  transfers between devices with their start and end apart: 8, of which 5 were waited for; matrix products, arithmetic and copies ran while one was open for 0% of the time, Pallas kernels for 3%

profile of v3, /device:TPU:1, one launch (start us, length us, event | category | flops | bytes accessed | tf_op | source)
XLA Modules:
  0.0 185.0 jit_solution(8252281208270159065)
XLA Ops:
  0.6 1.5 shard_map.85
  2.1 8.8 %collective-permute-start = (bf16[144,1024]{1,0:T(8,128)(2,1)S(1)}, bf16[144,1024]{1,0:T(8,128)(2,1)S(1)}, u32[]{:S(2)}, u32[]{:S(2)}) collective-permute-start(bf16[144,1024]{1,0:T(8,128)(2,1)S(1)} %get-tuple-element.39), channel_id=1, source_target_pairs={{0,16},{16,0},{1,17},{17,1},{2,18},{18,2},{3,19},{19,3},{4,20},{20... | collective-permute-start | bytes 884744 | tf_op jit(solution)/shard_map/ppermute | solution.py:25
  10.9 1.2 collective-permute-done.pack
  12.1 2.3 %collective-permute-start.3 = (bf16[96,128,128]{2,1,0:T(8,128)(2,1)}, bf16[96,128,128]{2,1,0:T(8,128)(2,1)}, u32[]{:S(2)}, u32[]{:S(2)}) collective-permute-start(bf16[96,128,128]{2,1,0:T(8,128)(2,1)} %own_in.1), channel_id=1, source_target_pairs={{0,16},{16,0},{1,17},{17,1},{2,18},{18,2},{3,19},{19,3},{4,20},{20... | collective-permute-start | bytes 9437192 | tf_op jit(solution)/shard_map/ppermute | solution.py:25
  14.4 0.1 conditional.2
  14.4 0.1 broadcast.2
  14.6 1.3 collective-permute-start.1
  15.9 16.5 %collective-permute-done.1 = bf16[128,128]{1,0:T(8,128)(2,1)S(1)} collective-permute-done((bf16[128,128]{1,0:T(8,128)(2,1)S(1)}, bf16[128,128]{1,0:T(8,128)(2,1)S(1)}, u32[]{:S(2)}, u32[]{:S(2)}) %collective-permute-start.1) | collective-permute-done | bytes 32800 | tf_op jit(solution)/shard_map/ppermute | solution.py:55
  32.3 14.6 %conditional.3 = (bf16[8,2,128,128]{3,2,1,0:T(8,128)(2,1)S(1)}) conditional(s32[]{:T(128)} %convert_element_type.11, (bf16[128,128]{1,0:T(8,128)(2,1)S(1)}, bf16[128,128]{1,0:T(8,128)(2,1)S(1)}) %tuple.26, bf16[8,2,128,128]{3,2,1,0:T(8,128)(2,1)S(1)} %get-tuple-element.59), branch_computations={%region_2.0_spmd, %region_3.0_spmd} | conditional | bytes 1048584 | solution.py:56
  32.3 0.1 branch_0_fun.1
  32.4 14.5 %all_to_all.39 = bf16[8,2,128,128]{3,2,1,0:T(8,128)(2,1)S(1)} all-to-all(bf16[8,2,128,128]{3,2,1,0:T(8,128)(2,1)S(1)} %branch_0_fun.1), channel_id=1, replica_groups=mesh['y'=8,'xl'=2,'core'=2,'xh'=2,'z'=8] {'y'}, dimensions={0} | all-to-all | bytes 1048576 | tf_op jit(solution)/shard_map/cond/branch_0_fun/all_to_all | solution.py:29
  47.0 0.0 copy-start.3
  47.0 2.2 %collective-permute-start.2 = (bf16[8,2,128,128]{3,2,1,0:T(8,128)(2,1)S(1)}, bf16[8,2,128,128]{3,2,1,0:T(8,128)(2,1)S(1)}, u32[]{:S(2)}, u32[]{:S(2)}) collective-permute-start(bf16[8,2,128,128]{3,2,1,0:T(8,128)(2,1)S(1)} %get-tuple-element.60.panels_in), channel_id=1, source_target_pairs={{0,32},{32,0},{1,33},{33,1},{2,34},{34,2},{3,35},{35,3},{4,36},{36... | collective-permute-start | bytes 1572872 | tf_op jit(solution)/shard_map/ppermute | solution.py:58
  49.2 0.1 pad_add_fusion.core_x
  49.3 0.0 collective-permute-done.3.other_in
  49.3 0.0 copy-done.3
  49.3 4.1 %shard_map.86 = (f32[2,17,128,128]{3,2,1,0:T(8,128)S(1)}, bf16[96,128,128]{2,1,0:T(8,128)(2,1)S(1)}, bf16[96,128,128]{2,1,0:T(8,128)(2,1)S(1)}) custom-call(s32[2]{0:T(128)S(1)} %pad_add_fusion.core_x, s32[1,96]{1,0:T(1,128)S(1)} %get-tuple-element.38.rows_own, s32[1,96]{1,0:T(1,128)S(1)} %slice_convert_fusion.rows_other, ...), custom_call_target="tpu_custom_call" | custom-call | flops 402653184 | bytes 6291456 | tf_op jit(solution)/shard_map/pallas_call | solution.py:290
  53.4 3.5 %collective-permute-done.2.panels = bf16[8,2,128,128]{3,2,1,0:T(8,128)(2,1)S(1)} collective-permute-done((bf16[8,2,128,128]{3,2,1,0:T(8,128)(2,1)S(1)}, bf16[8,2,128,128]{3,2,1,0:T(8,128)(2,1)S(1)}, u32[]{:S(2)}, u32[]{:S(2)}) %collective-permute-start.2) | collective-permute-done | bytes 524320 | tf_op jit(solution)/shard_map/ppermute | solution.py:58
  56.9 1.9 %shard_map.87 = bf16[16,2,128,128]{3,2,1,0:T(8,128)(2,1)S(1)} custom-call(s32[2]{0:T(128)S(1)} %pad_add_fusion.core_x, s32[1,96]{1,0:T(1,128)S(1)} %get-tuple-element.38.rows_own, s32[1,96]{1,0:T(1,128)S(1)} %slice_convert_fusion.rows_other, bf16[8,2,128,128]{3,2,1,0:T(8,128)(2,1)S(1)} %collective-permute-done.2.panels, ...), custom_call_target="tpu_custom_call" | custom-call | flops 402653184 | bytes 6291456 | tf_op jit(solution)/shard_map/pallas_call | solution.py:303
  58.8 32.1 %all_to_all.40.parts = bf16[16,2,128,128]{3,2,1,0:T(8,128)(2,1)S(1)} all-to-all(bf16[16,2,128,128]{3,2,1,0:T(8,128)(2,1)S(1)} %shard_map.87), channel_id=1, replica_groups=mesh['y'=8,'xl'=2,'core'=2,'xh'=2,'z'=8] {'xh','z'}, dimensions={0} | all-to-all | bytes 2097152 | tf_op jit(solution)/shard_map/all_to_all | solution.py:29
  90.9 0.4 shard_map.88
  91.3 23.8 %all_to_all.41.grads = bf16[16,2,128,128]{3,2,1,0:T(8,128)(2,1)S(1)} all-to-all(bf16[16,2,128,128]{3,2,1,0:T(8,128)(2,1)S(1)} %get-tuple-element.50), channel_id=1, replica_groups=mesh['y'=8,'xl'=2,'core'=2,'xh'=2,'z'=8] {'xh','z'}, dimensions={0} | all-to-all | bytes 2097152 | tf_op jit(solution)/shard_map/all_to_all | solution.py:29
  115.2 0.0 copy-start.1
  115.2 0.0 copy-start.2
  115.2 2.4 %shard_map.89 = bf16[16,2,128,128]{3,2,1,0:T(8,128)(2,1)S(1)} custom-call(s32[1]{0:T(128)} %bitcast.core, s32[1,96]{1,0:T(1,128)S(1)} %get-tuple-element.38.rows_own, s32[1,96]{1,0:T(1,128)S(1)} %slice_convert_fusion.rows_other, bf16[16,2,128,128]{3,2,1,0:T(8,128)(2,1)S(1)} %all_to_all.41.grads, bf16[96,128,128]{2,1,0:T(8,128)(2,1)S(1)} %get-tuple-element.45.own, ...), custom_call_target="tpu_custom_call" | custom-call | tf_op jit(solution)/shard_map/pallas_call | solution.py:324
  117.6 0.0 copy-start
  117.6 21.7 %all_to_all.42.parts = bf16[16,2,128,128]{3,2,1,0:T(8,128)(2,1)S(1)} all-to-all(bf16[16,2,128,128]{3,2,1,0:T(8,128)(2,1)S(1)} %shard_map.89), channel_id=1, replica_groups=mesh['y'=8,'xl'=2,'core'=2,'xh'=2,'z'=8] {'y','xl'}, dimensions={0} | all-to-all | bytes 2097152 | tf_op jit(solution)/shard_map/all_to_all | solution.py:29
  139.4 0.0 copy-done.1
  139.4 0.0 copy-done.2
  139.4 0.6 shard_map.90
  139.9 13.6 %all_to_all.43.parts = bf16[16,48,128]{2,1,0:T(8,128)(2,1)S(1)} all-to-all(bf16[16,48,128]{2,1,0:T(8,128)(2,1)S(1)} %bitcast.13), channel_id=1, replica_groups=mesh['y'=8,'xl'=2,'core'=2,'xh'=2,'z'=8] {'xh','z'}, dimensions={0} | all-to-all | bytes 393216 | tf_op jit(solution)/shard_map/all_to_all | solution.py:29
  153.5 0.7 shard_map.92
  154.3 3.5 %all-to-all-start.6 = ((bf16[16,48,128]{2,1,0:T(8,128)(2,1)}), bf16[16,48,128]{2,1,0:T(8,128)(2,1)S(1)}, u32[]{:S(2)}, u32[]{:S(2)}) async-start(bf16[16,48,128]{2,1,0:T(8,128)(2,1)} %shard_map.92), calls=%async_computation.6 | async-start | bytes 393216 | tf_op jit(solution)/shard_map/all_to_all | solution.py:29
  157.8 9.0 %all-to-all-done.6.parts = bf16[16,48,128]{2,1,0:T(8,128)(2,1)S(1)} async-done(((bf16[16,48,128]{2,1,0:T(8,128)(2,1)}), bf16[16,48,128]{2,1,0:T(8,128)(2,1)S(1)}, u32[]{:S(2)}, u32[]{:S(2)}) %all-to-all-start.6) | async-done | bytes 196640 | tf_op jit(solution)/shard_map/all_to_all | solution.py:29
  166.8 0.7 shard_map.93
  167.6 3.9 %all-to-all-start.7 = ((bf16[16,48,128]{2,1,0:T(8,128)(2,1)}), bf16[16,48,128]{2,1,0:T(8,128)(2,1)S(1)}, u32[]{:S(2)}, u32[]{:S(2)}) async-start(bf16[16,48,128]{2,1,0:T(8,128)(2,1)} %shard_map.93), calls=%async_computation.7 | async-start | bytes 393216 | tf_op jit(solution)/shard_map/all_to_all | solution.py:29
  171.5 1.9 %collective-permute-start.4 = (bf16[2,128,128]{2,1,0:T(8,128)(2,1)S(1)}, bf16[2,128,128]{2,1,0:T(8,128)(2,1)S(1)}, u32[]{:S(2)}, u32[]{:S(2)}) collective-permute-start(bf16[2,128,128]{2,1,0:T(8,128)(2,1)S(1)} %pad_maximum_fusion), channel_id=1, source_target_pairs={{0,16},{16,0},{1,17},{17,1},{2,18},{18,2},{3,19},{19,3},{4,20},{20... | collective-permute-start | bytes 196616 | tf_op jit(solution)/shard_map/ppermute | solution.py:25
  173.4 7.0 %all-to-all-done.7 = bf16[16,48,128]{2,1,0:T(8,128)(2,1)S(1)} async-done(((bf16[16,48,128]{2,1,0:T(8,128)(2,1)}), bf16[16,48,128]{2,1,0:T(8,128)(2,1)S(1)}, u32[]{:S(2)}, u32[]{:S(2)}) %all-to-all-start.7) | async-done | bytes 196640 | tf_op jit(solution)/shard_map/all_to_all | solution.py:29
  180.4 1.9 %collective-permute-start.5 = (bf16[768,128]{1,0:T(8,128)(2,1)S(1)}, bf16[768,128]{1,0:T(8,128)(2,1)S(1)}, u32[]{:S(2)}, u32[]{:S(2)}) collective-permute-start(bf16[768,128]{1,0:T(8,128)(2,1)S(1)} %bitcast.14), channel_id=1, source_target_pairs={{0,16},{16,0},{1,17},{17,1},{2,18},{18,2},{3,19},{19,3},{4,20},{20... | collective-permute-start | bytes 589832 | tf_op jit(solution)/shard_map/ppermute | solution.py:25
  182.4 0.0 collective-permute-done.4
  182.4 0.0 copy-done
  182.4 1.0 shard_map.91
  183.4 0.6 maximum_select_fusion.1
  184.0 0.0 collective-permute-done.5
  184.0 1.0 fusion
  (6 shorter events, 0.0 us)
Async XLA Ops:
  2.1 10.0 %collective-permute-start = (bf16[144,1024]{1,0:T(8,128)(2,1)S(1)}, bf16[144,1024]{1,0:T(8,128)(2,1)S(1)}, u32[]{:S(2)}, u32[]{:S(2)}) collective-permute-start(bf16[144,1024]{1,0:T(8,128)(2,1)S(1)} %get-tuple-element.39), channel_id=1, source_target_pairs={{0,16},{16,0},{1,17},{17,1},{2,18},{18,2},{3,19},{19,3},{4,20},{20... | collective-permute-start | bytes 884744 | tf_op jit(solution)/shard_map/ppermute | solution.py:25
  12.1 37.2 %collective-permute-start.3 = (bf16[96,128,128]{2,1,0:T(8,128)(2,1)}, bf16[96,128,128]{2,1,0:T(8,128)(2,1)}, u32[]{:S(2)}, u32[]{:S(2)}) collective-permute-start(bf16[96,128,128]{2,1,0:T(8,128)(2,1)} %own_in.1), channel_id=1, source_target_pairs={{0,16},{16,0},{1,17},{17,1},{2,18},{18,2},{3,19},{19,3},{4,20},{20... | collective-permute-start | bytes 9437192 | tf_op jit(solution)/shard_map/ppermute | solution.py:25
  14.6 17.8 %collective-permute-start.1 = (bf16[128,128]{1,0:T(8,128)(2,1)S(1)}, bf16[128,128]{1,0:T(8,128)(2,1)S(1)}, u32[]{:S(2)}, u32[]{:S(2)}) collective-permute-start(bf16[128,128]{1,0:T(8,128)(2,1)S(1)} %slice.29), channel_id=1, source_target_pairs={{0,16},{1,17},{2,18},{3,19},{4,20},{5,21},{6,22},{7,23},{8,24},{9,... | collective-permute-start | bytes 98312 | tf_op jit(solution)/shard_map/ppermute | solution.py:55
  47.0 2.3 %copy-start.3 = (bf16[8,2,128,128]{3,2,1,0:T(8,128)(2,1)}, bf16[8,2,128,128]{3,2,1,0:T(8,128)(2,1)S(1)}, u32[]{:S(2)}) copy-start(bf16[8,2,128,128]{3,2,1,0:T(8,128)(2,1)S(1)} %get-tuple-element.60.panels_in) | copy-start | bytes 1572868
  47.0 9.9 %collective-permute-start.2 = (bf16[8,2,128,128]{3,2,1,0:T(8,128)(2,1)S(1)}, bf16[8,2,128,128]{3,2,1,0:T(8,128)(2,1)S(1)}, u32[]{:S(2)}, u32[]{:S(2)}) collective-permute-start(bf16[8,2,128,128]{3,2,1,0:T(8,128)(2,1)S(1)} %get-tuple-element.60.panels_in), channel_id=1, source_target_pairs={{0,32},{32,0},{1,33},{33,1},{2,34},{34,2},{3,35},{35,3},{4,36},{36... | collective-permute-start | bytes 1572872 | tf_op jit(solution)/shard_map/ppermute | solution.py:58
  115.2 24.2 %copy-start.1 = (bf16[128,768]{1,0:T(8,128)(2,1)S(1)}, bf16[128,768]{1,0:T(8,128)(2,1)}, u32[]{:S(2)}) copy-start(bf16[128,768]{1,0:T(8,128)(2,1)} %features.3) | copy-start | bytes 589828
  115.2 24.2 %copy-start.2 = (s32[1,128]{1,0:T(1,128)S(1)}, s32[1,128]{1,0:T(1,128)}, u32[]{:S(2)}) copy-start(s32[1,128]{1,0:T(1,128)} %order.1) | copy-start | bytes 1540
  117.6 64.8 %copy-start = (bf16[768,256]{1,0:T(8,128)(2,1)S(1)}, bf16[768,256]{1,0:T(8,128)(2,1)}, u32[]{:S(2)}) copy-start(bf16[768,256]{1,0:T(8,128)(2,1)} %weight.1) | copy-start | bytes 1179652
  154.3 12.6 %all-to-all-start.6 = ((bf16[16,48,128]{2,1,0:T(8,128)(2,1)}), bf16[16,48,128]{2,1,0:T(8,128)(2,1)S(1)}, u32[]{:S(2)}, u32[]{:S(2)}) async-start(bf16[16,48,128]{2,1,0:T(8,128)(2,1)} %shard_map.92), calls=%async_computation.6 | async-start | bytes 393216 | tf_op jit(solution)/shard_map/all_to_all | solution.py:29
  167.6 12.9 %all-to-all-start.7 = ((bf16[16,48,128]{2,1,0:T(8,128)(2,1)}), bf16[16,48,128]{2,1,0:T(8,128)(2,1)S(1)}, u32[]{:S(2)}, u32[]{:S(2)}) async-start(bf16[16,48,128]{2,1,0:T(8,128)(2,1)} %shard_map.93), calls=%async_computation.7 | async-start | bytes 393216 | tf_op jit(solution)/shard_map/all_to_all | solution.py:29
  171.5 10.9 %collective-permute-start.4 = (bf16[2,128,128]{2,1,0:T(8,128)(2,1)S(1)}, bf16[2,128,128]{2,1,0:T(8,128)(2,1)S(1)}, u32[]{:S(2)}, u32[]{:S(2)}) collective-permute-start(bf16[2,128,128]{2,1,0:T(8,128)(2,1)S(1)} %pad_maximum_fusion), channel_id=1, source_target_pairs={{0,16},{16,0},{1,17},{17,1},{2,18},{18,2},{3,19},{19,3},{4,20},{20... | collective-permute-start | bytes 196616 | tf_op jit(solution)/shard_map/ppermute | solution.py:25
  180.4 3.6 %collective-permute-start.5 = (bf16[768,128]{1,0:T(8,128)(2,1)S(1)}, bf16[768,128]{1,0:T(8,128)(2,1)S(1)}, u32[]{:S(2)}, u32[]{:S(2)}) collective-permute-start(bf16[768,128]{1,0:T(8,128)(2,1)S(1)} %bitcast.14), channel_id=1, source_target_pairs={{0,16},{16,0},{1,17},{17,1},{2,18},{18,2},{3,19},{19,3},{4,20},{20... | collective-permute-start | bytes 589832 | tf_op jit(solution)/shard_map/ppermute | solution.py:25

commit v4 on v3

--- a/solution.py
+++ b/solution.py
@@ -34,6 +34,20 @@
         out[:, which] = jnp.broadcast_to(half[...][None], (out.shape[0],) + half.shape)
 
 
+def copy_kernel(source, target):
+    target[...] = source[...]
+
+
+def copied(value):
+    return pl.pallas_call(
+        copy_kernel,
+        out_shape=pltpu.HBM(value.shape, value.dtype),
+        in_specs=[VMEM],
+        out_specs=VMEM,
+        compiler_params=params(16),
+    )(in_hbm(value))
+
+
 def gathered_panels(mine, received, held, first, count):
     shape = (count, 2) + mine.shape
 
@@ -53,7 +67,7 @@
     panels = lax.cond(first, gather, skip, mine, received)
     panels, held = lax.optimization_barrier((panels, held))
     held = lax.ppermute(held, "core", [(0, 1)])
-    panels = lax.cond(first, lambda near, far, done: done,
+    panels = lax.cond(first, lambda near, far, done: copied(done),
                       lambda near, far, done: gather(near, far), mine, held, panels)
     return panels, lax.ppermute(panels, "xl", SWAP)
 

time: 186 us -> 184 us (0.989)
  blocking collectives: 106 us -> 104 us
where the time goes in v4:
time: 184 us; the launch traced here: 183 us
  blocking collectives  104 us (57%)
  waiting for transfers between devices  37.6 us (20%)
  starting transfers between devices  25.6 us (14%)
  Pallas kernels  13.4 us (7%)
    all_to_all x5, blocking collectives, exchange(): return lax.all_to_all(value, axes, 0, 0, tiled=True)  104 us
    ppermute x1, waiting for transfers between devices, gathered_panels(): held = lax.ppermute(held, 'core', [(0, 1)])  16.5 us
    all_to_all x2, waiting for transfers between devices, exchange(): return lax.all_to_all(value, axes, 0, 0, tiled=True)  16.2 us
    ppermute x4, starting transfers between devices, swap(): return lax.ppermute(value, 'core', SWAP)  14.9 us
    all_to_all x2, starting transfers between devices, exchange(): return lax.all_to_all(value, axes, 0, 0, tiled=True)  7.15 us
    pallas_call x1, Pallas kernels, per_device(): pl.pallas_call(near_kernel, out_shape=[jax.ShapeDtypeStruct(total_shape,...  4.08 us
    ppermute x1, waiting for transfers between devices, gathered_panels(): return (panels, lax.ppermute(panels, 'xl', SWAP))  3.71 us
  transfers between devices with their start and end apart: 8, of which 5 were waited for; matrix products, arithmetic and copies ran while one was open for 0% of the time, Pallas kernels for 3%

profile of v4, /device:TPU:1, one launch (start us, length us, event | category | flops | bytes accessed | tf_op | source)
XLA Modules:
  0.0 183.4 jit_solution(10108518775920493480)
XLA Ops:
  0.6 1.5 shard_map.85
  2.1 8.8 %collective-permute-start = (bf16[144,1024]{1,0:T(8,128)(2,1)S(1)}, bf16[144,1024]{1,0:T(8,128)(2,1)S(1)}, u32[]{:S(2)}, u32[]{:S(2)}) collective-permute-start(bf16[144,1024]{1,0:T(8,128)(2,1)S(1)} %get-tuple-element.39), channel_id=1, source_target_pairs={{0,16},{16,0},{1,17},{17,1},{2,18},{18,2},{3,19},{19,3},{4,20},{20... | collective-permute-start | bytes 884744 | tf_op jit(solution)/shard_map/ppermute | solution.py:25
  10.9 1.2 collective-permute-done.pack
  12.1 2.3 %collective-permute-start.3 = (bf16[96,128,128]{2,1,0:T(8,128)(2,1)}, bf16[96,128,128]{2,1,0:T(8,128)(2,1)}, u32[]{:S(2)}, u32[]{:S(2)}) collective-permute-start(bf16[96,128,128]{2,1,0:T(8,128)(2,1)} %own_in.1), channel_id=1, source_target_pairs={{0,16},{16,0},{1,17},{17,1},{2,18},{18,2},{3,19},{19,3},{4,20},{20... | collective-permute-start | bytes 9437192 | tf_op jit(solution)/shard_map/ppermute | solution.py:25
  14.4 0.1 conditional.2
  14.4 0.1 broadcast.2
  14.6 1.3 collective-permute-start.1
  15.9 16.5 %collective-permute-done.1 = bf16[128,128]{1,0:T(8,128)(2,1)S(1)} collective-permute-done((bf16[128,128]{1,0:T(8,128)(2,1)S(1)}, bf16[128,128]{1,0:T(8,128)(2,1)S(1)}, u32[]{:S(2)}, u32[]{:S(2)}) %collective-permute-start.1) | collective-permute-done | bytes 32800 | tf_op jit(solution)/shard_map/ppermute | solution.py:69
  32.3 15.3 %conditional.3 = (bf16[8,2,128,128]{3,2,1,0:T(8,128)(2,1)}) conditional(s32[]{:T(128)} %convert_element_type.11, (bf16[128,128]{1,0:T(8,128)(2,1)S(1)}, bf16[128,128]{1,0:T(8,128)(2,1)S(1)}) %tuple.26, bf16[8,2,128,128]{3,2,1,0:T(8,128)(2,1)S(1)} %get-tuple-element.59), branch_computations={%region_2.0_spmd, %region_3.0_spmd} | conditional | bytes 2097188 | solution.py:70
  32.3 0.1 branch_0_fun.1
  32.4 15.2 %all_to_all.39 = bf16[8,2,128,128]{3,2,1,0:T(8,128)(2,1)} all-to-all(bf16[8,2,128,128]{3,2,1,0:T(8,128)(2,1)S(1)} %branch_0_fun.1), channel_id=1, replica_groups=mesh['y'=8,'xl'=2,'core'=2,'xh'=2,'z'=8] {'y'}, dimensions={0} | all-to-all | bytes 1048576 | tf_op jit(solution)/shard_map/cond/branch_0_fun/all_to_all | solution.py:29
  47.6 2.2 %collective-permute-start.2 = (bf16[8,2,128,128]{3,2,1,0:T(8,128)(2,1)}, bf16[8,2,128,128]{3,2,1,0:T(8,128)(2,1)S(1)}, u32[]{:S(2)}, u32[]{:S(2)}) collective-permute-start(bf16[8,2,128,128]{3,2,1,0:T(8,128)(2,1)} %get-tuple-element.60.panels_in), channel_id=1, source_target_pairs={{0,32},{32,0},{1,33},{33,1},{2,34},{34,2},{3,35},{35,3},{4,36},{36... | collective-permute-start | bytes 1572872 | tf_op jit(solution)/shard_map/ppermute | solution.py:72
  49.9 0.1 pad_add_fusion.core_x
  50.0 0.0 collective-permute-done.3.other_in
  50.0 4.1 %shard_map.86 = (f32[2,17,128,128]{3,2,1,0:T(8,128)S(1)}, bf16[96,128,128]{2,1,0:T(8,128)(2,1)S(1)}, bf16[96,128,128]{2,1,0:T(8,128)(2,1)S(1)}) custom-call(s32[2]{0:T(128)S(1)} %pad_add_fusion.core_x, s32[1,96]{1,0:T(1,128)S(1)} %get-tuple-element.38.rows_own, s32[1,96]{1,0:T(1,128)S(1)} %slice_convert_fusion.rows_other, ...), custom_call_target="tpu_custom_call" | custom-call | flops 402653184 | bytes 6291456 | tf_op jit(solution)/shard_map/pallas_call | solution.py:304
  54.1 3.7 %collective-permute-done.2.panels = bf16[8,2,128,128]{3,2,1,0:T(8,128)(2,1)S(1)} collective-permute-done((bf16[8,2,128,128]{3,2,1,0:T(8,128)(2,1)}, bf16[8,2,128,128]{3,2,1,0:T(8,128)(2,1)S(1)}, u32[]{:S(2)}, u32[]{:S(2)}) %collective-permute-start.2) | collective-permute-done | bytes 524320 | tf_op jit(solution)/shard_map/ppermute | solution.py:72
  57.8 1.9 %shard_map.87 = bf16[16,2,128,128]{3,2,1,0:T(8,128)(2,1)S(1)} custom-call(s32[2]{0:T(128)S(1)} %pad_add_fusion.core_x, s32[1,96]{1,0:T(1,128)S(1)} %get-tuple-element.38.rows_own, s32[1,96]{1,0:T(1,128)S(1)} %slice_convert_fusion.rows_other, bf16[8,2,128,128]{3,2,1,0:T(8,128)(2,1)S(1)} %collective-permute-done.2.panels, ...), custom_call_target="tpu_custom_call" | custom-call | flops 402653184 | bytes 6291456 | tf_op jit(solution)/shard_map/pallas_call | solution.py:317
  59.7 29.7 %all_to_all.40.parts = bf16[16,2,128,128]{3,2,1,0:T(8,128)(2,1)S(1)} all-to-all(bf16[16,2,128,128]{3,2,1,0:T(8,128)(2,1)S(1)} %shard_map.87), channel_id=1, replica_groups=mesh['y'=8,'xl'=2,'core'=2,'xh'=2,'z'=8] {'xh','z'}, dimensions={0} | all-to-all | bytes 2097152 | tf_op jit(solution)/shard_map/all_to_all | solution.py:29
  89.4 0.4 shard_map.88
  89.8 23.2 %all_to_all.41.grads = bf16[16,2,128,128]{3,2,1,0:T(8,128)(2,1)S(1)} all-to-all(bf16[16,2,128,128]{3,2,1,0:T(8,128)(2,1)S(1)} %get-tuple-element.50), channel_id=1, replica_groups=mesh['y'=8,'xl'=2,'core'=2,'xh'=2,'z'=8] {'xh','z'}, dimensions={0} | all-to-all | bytes 2097152 | tf_op jit(solution)/shard_map/all_to_all | solution.py:29
  113.0 0.0 copy-start.1
  113.0 0.0 copy-start.2
  113.0 2.4 %shard_map.89 = bf16[16,2,128,128]{3,2,1,0:T(8,128)(2,1)S(1)} custom-call(s32[1]{0:T(128)} %bitcast.core, s32[1,96]{1,0:T(1,128)S(1)} %get-tuple-element.38.rows_own, s32[1,96]{1,0:T(1,128)S(1)} %slice_convert_fusion.rows_other, bf16[16,2,128,128]{3,2,1,0:T(8,128)(2,1)S(1)} %all_to_all.41.grads, bf16[96,128,128]{2,1,0:T(8,128)(2,1)S(1)} %get-tuple-element.45.own, ...), custom_call_target="tpu_custom_call" | custom-call | tf_op jit(solution)/shard_map/pallas_call | solution.py:338
  115.4 0.0 copy-start
  115.5 22.8 %all_to_all.42.parts = bf16[16,2,128,128]{3,2,1,0:T(8,128)(2,1)S(1)} all-to-all(bf16[16,2,128,128]{3,2,1,0:T(8,128)(2,1)S(1)} %shard_map.89), channel_id=1, replica_groups=mesh['y'=8,'xl'=2,'core'=2,'xh'=2,'z'=8] {'y','xl'}, dimensions={0} | all-to-all | bytes 2097152 | tf_op jit(solution)/shard_map/all_to_all | solution.py:29
  138.2 0.0 copy-done.1
  138.2 0.0 copy-done.2
  138.2 0.6 shard_map.90
  138.8 13.2 %all_to_all.43.parts = bf16[16,48,128]{2,1,0:T(8,128)(2,1)S(1)} all-to-all(bf16[16,48,128]{2,1,0:T(8,128)(2,1)S(1)} %bitcast.13), channel_id=1, replica_groups=mesh['y'=8,'xl'=2,'core'=2,'xh'=2,'z'=8] {'xh','z'}, dimensions={0} | all-to-all | bytes 393216 | tf_op jit(solution)/shard_map/all_to_all | solution.py:29
  152.0 0.7 shard_map.92
  152.7 3.5 %all-to-all-start.6 = ((bf16[16,48,128]{2,1,0:T(8,128)(2,1)}), bf16[16,48,128]{2,1,0:T(8,128)(2,1)S(1)}, u32[]{:S(2)}, u32[]{:S(2)}) async-start(bf16[16,48,128]{2,1,0:T(8,128)(2,1)} %shard_map.92), calls=%async_computation.6 | async-start | bytes 393216 | tf_op jit(solution)/shard_map/all_to_all | solution.py:29
  156.3 9.0 %all-to-all-done.6.parts = bf16[16,48,128]{2,1,0:T(8,128)(2,1)S(1)} async-done(((bf16[16,48,128]{2,1,0:T(8,128)(2,1)}), bf16[16,48,128]{2,1,0:T(8,128)(2,1)S(1)}, u32[]{:S(2)}, u32[]{:S(2)}) %all-to-all-start.6) | async-done | bytes 196640 | tf_op jit(solution)/shard_map/all_to_all | solution.py:29
  165.3 0.7 shard_map.93
  166.0 3.6 %all-to-all-start.7 = ((bf16[16,48,128]{2,1,0:T(8,128)(2,1)}), bf16[16,48,128]{2,1,0:T(8,128)(2,1)S(1)}, u32[]{:S(2)}, u32[]{:S(2)}) async-start(bf16[16,48,128]{2,1,0:T(8,128)(2,1)} %shard_map.93), calls=%async_computation.7 | async-start | bytes 393216 | tf_op jit(solution)/shard_map/all_to_all | solution.py:29
  169.7 1.9 %collective-permute-start.4 = (bf16[2,128,128]{2,1,0:T(8,128)(2,1)S(1)}, bf16[2,128,128]{2,1,0:T(8,128)(2,1)S(1)}, u32[]{:S(2)}, u32[]{:S(2)}) collective-permute-start(bf16[2,128,128]{2,1,0:T(8,128)(2,1)S(1)} %pad_maximum_fusion), channel_id=1, source_target_pairs={{0,16},{16,0},{1,17},{17,1},{2,18},{18,2},{3,19},{19,3},{4,20},{20... | collective-permute-start | bytes 196616 | tf_op jit(solution)/shard_map/ppermute | solution.py:25
  171.6 7.2 %all-to-all-done.7 = bf16[16,48,128]{2,1,0:T(8,128)(2,1)S(1)} async-done(((bf16[16,48,128]{2,1,0:T(8,128)(2,1)}), bf16[16,48,128]{2,1,0:T(8,128)(2,1)S(1)}, u32[]{:S(2)}, u32[]{:S(2)}) %all-to-all-start.7) | async-done | bytes 196640 | tf_op jit(solution)/shard_map/all_to_all | solution.py:29
  178.8 1.9 %collective-permute-start.5 = (bf16[768,128]{1,0:T(8,128)(2,1)S(1)}, bf16[768,128]{1,0:T(8,128)(2,1)S(1)}, u32[]{:S(2)}, u32[]{:S(2)}) collective-permute-start(bf16[768,128]{1,0:T(8,128)(2,1)S(1)} %bitcast.14), channel_id=1, source_target_pairs={{0,16},{16,0},{1,17},{17,1},{2,18},{18,2},{3,19},{19,3},{4,20},{20... | collective-permute-start | bytes 589832 | tf_op jit(solution)/shard_map/ppermute | solution.py:25
  180.7 0.0 collective-permute-done.4
  180.7 0.0 copy-done
  180.8 1.0 shard_map.91
  181.7 0.6 maximum_select_fusion.1
  182.4 0.0 collective-permute-done.5
  182.4 1.0 fusion
  (6 shorter events, 0.0 us)
Async XLA Ops:
  2.1 10.0 %collective-permute-start = (bf16[144,1024]{1,0:T(8,128)(2,1)S(1)}, bf16[144,1024]{1,0:T(8,128)(2,1)S(1)}, u32[]{:S(2)}, u32[]{:S(2)}) collective-permute-start(bf16[144,1024]{1,0:T(8,128)(2,1)S(1)} %get-tuple-element.39), channel_id=1, source_target_pairs={{0,16},{16,0},{1,17},{17,1},{2,18},{18,2},{3,19},{19,3},{4,20},{20... | collective-permute-start | bytes 884744 | tf_op jit(solution)/shard_map/ppermute | solution.py:25
  12.1 37.8 %collective-permute-start.3 = (bf16[96,128,128]{2,1,0:T(8,128)(2,1)}, bf16[96,128,128]{2,1,0:T(8,128)(2,1)}, u32[]{:S(2)}, u32[]{:S(2)}) collective-permute-start(bf16[96,128,128]{2,1,0:T(8,128)(2,1)} %own_in.1), channel_id=1, source_target_pairs={{0,16},{16,0},{1,17},{17,1},{2,18},{18,2},{3,19},{19,3},{4,20},{20... | collective-permute-start | bytes 9437192 | tf_op jit(solution)/shard_map/ppermute | solution.py:25
  14.6 17.8 %collective-permute-start.1 = (bf16[128,128]{1,0:T(8,128)(2,1)S(1)}, bf16[128,128]{1,0:T(8,128)(2,1)S(1)}, u32[]{:S(2)}, u32[]{:S(2)}) collective-permute-start(bf16[128,128]{1,0:T(8,128)(2,1)S(1)} %slice.29), channel_id=1, source_target_pairs={{0,16},{1,17},{2,18},{3,19},{4,20},{5,21},{6,22},{7,23},{8,24},{9,... | collective-permute-start | bytes 98312 | tf_op jit(solution)/shard_map/ppermute | solution.py:69
  47.6 10.1 %collective-permute-start.2 = (bf16[8,2,128,128]{3,2,1,0:T(8,128)(2,1)}, bf16[8,2,128,128]{3,2,1,0:T(8,128)(2,1)S(1)}, u32[]{:S(2)}, u32[]{:S(2)}) collective-permute-start(bf16[8,2,128,128]{3,2,1,0:T(8,128)(2,1)} %get-tuple-element.60.panels_in), channel_id=1, source_target_pairs={{0,32},{32,0},{1,33},{33,1},{2,34},{34,2},{3,35},{35,3},{4,36},{36... | collective-permute-start | bytes 1572872 | tf_op jit(solution)/shard_map/ppermute | solution.py:72
  113.0 25.2 %copy-start.1 = (bf16[128,768]{1,0:T(8,128)(2,1)S(1)}, bf16[128,768]{1,0:T(8,128)(2,1)}, u32[]{:S(2)}) copy-start(bf16[128,768]{1,0:T(8,128)(2,1)} %features.3) | copy-start | bytes 589828
  113.0 25.2 %copy-start.2 = (s32[1,128]{1,0:T(1,128)S(1)}, s32[1,128]{1,0:T(1,128)}, u32[]{:S(2)}) copy-start(s32[1,128]{1,0:T(1,128)} %order.1) | copy-start | bytes 1540
  115.4 65.3 %copy-start = (bf16[768,256]{1,0:T(8,128)(2,1)S(1)}, bf16[768,256]{1,0:T(8,128)(2,1)}, u32[]{:S(2)}) copy-start(bf16[768,256]{1,0:T(8,128)(2,1)} %weight.1) | copy-start | bytes 1179652
  152.7 12.6 %all-to-all-start.6 = ((bf16[16,48,128]{2,1,0:T(8,128)(2,1)}), bf16[16,48,128]{2,1,0:T(8,128)(2,1)S(1)}, u32[]{:S(2)}, u32[]{:S(2)}) async-start(bf16[16,48,128]{2,1,0:T(8,128)(2,1)} %shard_map.92), calls=%async_computation.6 | async-start | bytes 393216 | tf_op jit(solution)/shard_map/all_to_all | solution.py:29
  166.0 12.8 %all-to-all-start.7 = ((bf16[16,48,128]{2,1,0:T(8,128)(2,1)}), bf16[16,48,128]{2,1,0:T(8,128)(2,1)S(1)}, u32[]{:S(2)}, u32[]{:S(2)}) async-start(bf16[16,48,128]{2,1,0:T(8,128)(2,1)} %shard_map.93), calls=%async_computation.7 | async-start | bytes 393216 | tf_op jit(solution)/shard_map/all_to_all | solution.py:29
  169.7 11.1 %collective-permute-start.4 = (bf16[2,128,128]{2,1,0:T(8,128)(2,1)S(1)}, bf16[2,128,128]{2,1,0:T(8,128)(2,1)S(1)}, u32[]{:S(2)}, u32[]{:S(2)}) collective-permute-start(bf16[2,128,128]{2,1,0:T(8,128)(2,1)S(1)} %pad_maximum_fusion), channel_id=1, source_target_pairs={{0,16},{16,0},{1,17},{17,1},{2,18},{18,2},{3,19},{19,3},{4,20},{20... | collective-permute-start | bytes 196616 | tf_op jit(solution)/shard_map/ppermute | solution.py:25
  178.8 3.6 %collective-permute-start.5 = (bf16[768,128]{1,0:T(8,128)(2,1)S(1)}, bf16[768,128]{1,0:T(8,128)(2,1)S(1)}, u32[]{:S(2)}, u32[]{:S(2)}) collective-permute-start(bf16[768,128]{1,0:T(8,128)(2,1)S(1)} %bitcast.14), channel_id=1, source_target_pairs={{0,16},{16,0},{1,17},{17,1},{2,18},{18,2},{3,19},{19,3},{4,20},{20... | collective-permute-start | bytes 589832 | tf_op jit(solution)/shard_map/ppermute | solution.py:25

commit v5 on v4

--- a/solution.py
+++ b/solution.py
@@ -231,7 +231,7 @@
         out[group // 2, (group % 2) ^ me] = dot(left, right, ((1,), (0,))).astype(BF16)
 
 
-def weight_kernel(scale, parts, order, features, pack, turned, term):
+def weight_kernel(scale, parts, order, features, pack, hidden, turned, late, term):
     size = features.shape[0]
     hid = pack.shape[1] - features.shape[1]
     order_other = pack[size:, :size][:1].astype(F32).astype(jnp.int32)
@@ -240,18 +240,25 @@
     for which, (source, values) in enumerate(both):
         panel_grad = jnp.sum(parts[:, which].astype(F32), axis=0).astype(BF16)
         placed = dot(panel_grad, source_onehot(source), ((1,), (1,))).astype(BF16)
-        turned[which] = placed
+        if which == 0:
+            turned[...] = placed
+        else:
+            late[1] = placed
         total = total + dot(placed, values, ((1,), (0,)))
+    late[0] = hidden[1]
     term[...] = (total * scale).T.astype(BF16)
 
 
-def feature_kernel(core, mine, theirs, weight, out):
+def feature_kernel(core, mine, late, hidden_pair, weight, out, hidden):
     half = mine.shape[0]
     me = core[0]
-    near = weight[:, pl.ds(pl.multiple_of(me * half, half), half)]
-    far = weight[:, pl.ds(pl.multiple_of((1 - me) * half, half), half)]
-    total = dot(mine[...], near, ((0,), (1,))) + dot(theirs[...], far, ((0,), (1,)))
+    near = pl.ds(pl.multiple_of(me * half, half), half)
+    far = pl.ds(pl.multiple_of((1 - me) * half, half), half)
+    total = dot(mine[...], weight[:, near], ((0,), (1,)))
+    total = total + dot(late[1], weight[:, far], ((0,), (1,)))
     out[...] = total.astype(BF16)
+    hidden[:, near] = hidden_pair[0]
+    hidden[:, far] = late[0]
 
 
 def per_device(features, node_order, weight, cotangent, tile_list, tile_values):
@@ -343,16 +350,17 @@
         compiler_params=params(24),
     )(core, rows_own, rows_other, grads, tiles_own, tiles_other)
     parts = exchange(contribution, CHIPS)
-    turned, term = pl.pallas_call(
+    turned, late, term = pl.pallas_call(
         functools.partial(weight_kernel, nodes ** -0.5),
         out_shape=[
-            jax.ShapeDtypeStruct((2, half, size), BF16),
+            jax.ShapeDtypeStruct((half, size), BF16),
+            jax.ShapeDtypeStruct((2, size, half), BF16),
             jax.ShapeDtypeStruct((in_width, half), BF16),
         ],
-        in_specs=[VMEM] * 4,
-        out_specs=[VMEM] * 2,
-        compiler_params=params(16),
-    )(parts, node_order, features, pack)
+        in_specs=[VMEM] * 5,
+        out_specs=[VMEM] * 3,
+        compiler_params=params(16),
+    )(parts, node_order, features, pack, hidden_pair)
 
     share = in_width // ranges
     term = exchange(term.reshape(ranges, share, half), COLS)
@@ -361,15 +369,16 @@
     term = term.reshape(in_width, half)
     weight_grad = joined(term, swap(term)).astype(F32)
 
-    late = swap(jnp.stack([hidden_pair[1], turned[1]]))
-    hidden = joined(hidden_pair[0], late[0])
-    x_grad = pl.pallas_call(
+    x_grad, hidden = pl.pallas_call(
         feature_kernel,
-        out_shape=jax.ShapeDtypeStruct((size, in_width), BF16),
-        in_specs=[SMEM, VMEM, VMEM, VMEM],
-        out_specs=VMEM,
-        compiler_params=params(16),
-    )(core, turned[0], late[1], weight)
+        out_shape=[
+            jax.ShapeDtypeStruct((size, in_width), BF16),
+            jax.ShapeDtypeStruct((size, hid), BF16),
+        ],
+        in_specs=[SMEM, VMEM, VMEM, VMEM, VMEM],
+        out_specs=[VMEM] * 2,
+        compiler_params=params(16),
+    )(core, turned, swap(late), hidden_pair, weight)
     return (hidden, x_grad, weight_grad)
 
 

time: 184 us -> 184 us (level)
  blocking collectives: 104 us -> 128 us
  waiting for transfers between devices: 37.6 us -> 22.3 us
  starting transfers between devices: 25.6 us -> 18.9 us
    all_to_all x5 -> x7, blocking collectives: 104 us -> 128 us  [exchange(): return lax.all_to_all(value, axes, 0, 0, tiled=True)]
    all_to_all x2 -> x0, waiting for transfers between devices: 16.2 us -> none  [exchange(): return lax.all_to_all(value, axes, 0, 0, tiled=True)]
    all_to_all x2 -> x0, starting transfers between devices: 7.15 us -> none  [exchange(): return lax.all_to_all(value, axes, 0, 0, tiled=True)]
  transfers between devices with their start and end apart: 8 -> 6, of which waited for: 5 -> 4; matrix products, arithmetic and copies ran while one was open for 0% -> 0% of each run, Pallas kernels for 3% -> 3%
where the time goes in v5:
time: 184 us
  blocking collectives  128 us (70%)
  waiting for transfers between devices  22.3 us (12%)
  starting transfers between devices  18.9 us (10%)
  Pallas kernels  12 us (7%)
    all_to_all x7, blocking collectives, exchange(): return lax.all_to_all(value, axes, 0, 0, tiled=True)  128 us
    ppermute x1, waiting for transfers between devices, gathered_panels(): held = lax.ppermute(held, 'core', [(0, 1)])  16.5 us
    ppermute x4, starting transfers between devices, swap(): return lax.ppermute(value, 'core', SWAP)  15.4 us
    pallas_call x1, Pallas kernels, per_device(): pl.pallas_call(near_kernel, out_shape=[jax.ShapeDtypeStruct(total_shape,...  4.08 us
    ppermute x1, waiting for transfers between devices, gathered_panels(): return (panels, lax.ppermute(panels, 'xl', SWAP))  3.71 us
  transfers between devices with their start and end apart: 6, of which 4 were waited for; matrix products, arithmetic and copies ran while one was open for 0% of the time, Pallas kernels for 3%

profile of v5, /device:TPU:1, one launch (start us, length us, event | category | flops | bytes accessed | tf_op | source)
XLA Modules:
  0.0 183.7 jit_solution(12046892683038401588)
XLA Ops:
  0.6 1.5 shard_map.85
  2.1 8.8 %collective-permute-start = (bf16[144,1024]{1,0:T(8,128)(2,1)S(1)}, bf16[144,1024]{1,0:T(8,128)(2,1)S(1)}, u32[]{:S(2)}, u32[]{:S(2)}) collective-permute-start(bf16[144,1024]{1,0:T(8,128)(2,1)S(1)} %get-tuple-element.42), channel_id=1, source_target_pairs={{0,16},{16,0},{1,17},{17,1},{2,18},{18,2},{3,19},{19,3},{4,20},{20... | collective-permute-start | bytes 884744 | tf_op jit(solution)/shard_map/ppermute | solution.py:25
  10.9 1.2 collective-permute-done.pack
  12.1 2.3 %collective-permute-start.3 = (bf16[96,128,128]{2,1,0:T(8,128)(2,1)}, bf16[96,128,128]{2,1,0:T(8,128)(2,1)}, u32[]{:S(2)}, u32[]{:S(2)}) collective-permute-start(bf16[96,128,128]{2,1,0:T(8,128)(2,1)} %own_in.1), channel_id=1, source_target_pairs={{0,16},{16,0},{1,17},{17,1},{2,18},{18,2},{3,19},{19,3},{4,20},{20... | collective-permute-start | bytes 9437192 | tf_op jit(solution)/shard_map/ppermute | solution.py:25
  14.4 0.1 conditional.2
  14.4 0.1 broadcast.2
  14.6 1.3 collective-permute-start.1
  15.9 16.5 %collective-permute-done.1 = bf16[128,128]{1,0:T(8,128)(2,1)S(1)} collective-permute-done((bf16[128,128]{1,0:T(8,128)(2,1)S(1)}, bf16[128,128]{1,0:T(8,128)(2,1)S(1)}, u32[]{:S(2)}, u32[]{:S(2)}) %collective-permute-start.1) | collective-permute-done | bytes 32800 | tf_op jit(solution)/shard_map/ppermute | solution.py:69
  32.3 15.3 %conditional.3 = (bf16[8,2,128,128]{3,2,1,0:T(8,128)(2,1)}) conditional(s32[]{:T(128)} %convert_element_type.11, (bf16[128,128]{1,0:T(8,128)(2,1)S(1)}, bf16[128,128]{1,0:T(8,128)(2,1)S(1)}) %tuple.26, bf16[8,2,128,128]{3,2,1,0:T(8,128)(2,1)S(1)} %get-tuple-element.59), branch_computations={%region_2.0_spmd, %region_3.0_spmd} | conditional | bytes 2097188 | solution.py:70
  32.3 0.1 branch_0_fun.1
  32.4 15.2 %all_to_all.39 = bf16[8,2,128,128]{3,2,1,0:T(8,128)(2,1)} all-to-all(bf16[8,2,128,128]{3,2,1,0:T(8,128)(2,1)S(1)} %branch_0_fun.1), channel_id=1, replica_groups=mesh['y'=8,'xl'=2,'core'=2,'xh'=2,'z'=8] {'y'}, dimensions={0} | all-to-all | bytes 1048576 | tf_op jit(solution)/shard_map/cond/branch_0_fun/all_to_all | solution.py:29
  47.7 2.2 %collective-permute-start.2 = (bf16[8,2,128,128]{3,2,1,0:T(8,128)(2,1)}, bf16[8,2,128,128]{3,2,1,0:T(8,128)(2,1)S(1)}, u32[]{:S(2)}, u32[]{:S(2)}) collective-permute-start(bf16[8,2,128,128]{3,2,1,0:T(8,128)(2,1)} %get-tuple-element.60.panels_in), channel_id=1, source_target_pairs={{0,32},{32,0},{1,33},{33,1},{2,34},{34,2},{3,35},{35,3},{4,36},{36... | collective-permute-start | bytes 1572872 | tf_op jit(solution)/shard_map/ppermute | solution.py:72
  49.9 0.1 pad_add_fusion.core_x
  50.0 0.0 collective-permute-done.3.other_in
  50.0 4.1 %shard_map.86 = (f32[2,17,128,128]{3,2,1,0:T(8,128)S(1)}, bf16[96,128,128]{2,1,0:T(8,128)(2,1)S(1)}, bf16[96,128,128]{2,1,0:T(8,128)(2,1)S(1)}) custom-call(s32[2]{0:T(128)S(1)} %pad_add_fusion.core_x, s32[1,96]{1,0:T(1,128)S(1)} %get-tuple-element.41.rows_own, s32[1,96]{1,0:T(1,128)S(1)} %slice_convert_fusion.rows_other, ...), custom_call_target="tpu_custom_call" | custom-call | flops 402653184 | bytes 6291456 | tf_op jit(solution)/shard_map/pallas_call | solution.py:311
  54.1 3.7 %collective-permute-done.2.panels = bf16[8,2,128,128]{3,2,1,0:T(8,128)(2,1)S(1)} collective-permute-done((bf16[8,2,128,128]{3,2,1,0:T(8,128)(2,1)}, bf16[8,2,128,128]{3,2,1,0:T(8,128)(2,1)S(1)}, u32[]{:S(2)}, u32[]{:S(2)}) %collective-permute-start.2) | collective-permute-done | bytes 524320 | tf_op jit(solution)/shard_map/ppermute | solution.py:72
  57.8 1.9 %shard_map.87 = bf16[16,2,128,128]{3,2,1,0:T(8,128)(2,1)S(1)} custom-call(s32[2]{0:T(128)S(1)} %pad_add_fusion.core_x, s32[1,96]{1,0:T(1,128)S(1)} %get-tuple-element.41.rows_own, s32[1,96]{1,0:T(1,128)S(1)} %slice_convert_fusion.rows_other, bf16[8,2,128,128]{3,2,1,0:T(8,128)(2,1)S(1)} %collective-permute-done.2.panels, ...), custom_call_target="tpu_custom_call" | custom-call | flops 402653184 | bytes 6291456 | tf_op jit(solution)/shard_map/pallas_call | solution.py:324
  59.7 29.8 %all_to_all.40.parts = bf16[16,2,128,128]{3,2,1,0:T(8,128)(2,1)S(1)} all-to-all(bf16[16,2,128,128]{3,2,1,0:T(8,128)(2,1)S(1)} %shard_map.87), channel_id=1, replica_groups=mesh['y'=8,'xl'=2,'core'=2,'xh'=2,'z'=8] {'xh','z'}, dimensions={0} | all-to-all | bytes 2097152 | tf_op jit(solution)/shard_map/all_to_all | solution.py:29
  89.5 0.4 shard_map.88
  89.9 23.5 %all_to_all.41.grads = bf16[16,2,128,128]{3,2,1,0:T(8,128)(2,1)S(1)} all-to-all(bf16[16,2,128,128]{3,2,1,0:T(8,128)(2,1)S(1)} %get-tuple-element.52), channel_id=1, replica_groups=mesh['y'=8,'xl'=2,'core'=2,'xh'=2,'z'=8] {'xh','z'}, dimensions={0} | all-to-all | bytes 2097152 | tf_op jit(solution)/shard_map/all_to_all | solution.py:29
  113.3 0.0 copy-start.1
  113.3 0.0 copy-start.2
  113.3 2.4 %shard_map.89 = bf16[16,2,128,128]{3,2,1,0:T(8,128)(2,1)S(1)} custom-call(s32[1]{0:T(128)} %bitcast.core, s32[1,96]{1,0:T(1,128)S(1)} %get-tuple-element.41.rows_own, s32[1,96]{1,0:T(1,128)S(1)} %slice_convert_fusion.rows_other, bf16[16,2,128,128]{3,2,1,0:T(8,128)(2,1)S(1)} %all_to_all.41.grads, bf16[96,128,128]{2,1,0:T(8,128)(2,1)S(1)} %get-tuple-element.48.own, ...), custom_call_target="tpu_custom_call" | custom-call | tf_op jit(solution)/shard_map/pallas_call | solution.py:345
  115.8 0.0 copy-start
  115.8 22.8 %all_to_all.42.parts = bf16[16,2,128,128]{3,2,1,0:T(8,128)(2,1)S(1)} all-to-all(bf16[16,2,128,128]{3,2,1,0:T(8,128)(2,1)S(1)} %shard_map.89), channel_id=1, replica_groups=mesh['y'=8,'xl'=2,'core'=2,'xh'=2,'z'=8] {'y','xl'}, dimensions={0} | all-to-all | bytes 2097152 | tf_op jit(solution)/shard_map/all_to_all | solution.py:29
  138.6 0.0 copy-done.1
  138.6 0.0 copy-done.2
  138.6 0.6 shard_map.90
  139.2 12.9 %all_to_all.43.parts = bf16[16,48,128]{2,1,0:T(8,128)(2,1)S(1)} all-to-all(bf16[16,48,128]{2,1,0:T(8,128)(2,1)S(1)} %bitcast.5), channel_id=1, replica_groups=mesh['y'=8,'xl'=2,'core'=2,'xh'=2,'z'=8] {'xh','z'}, dimensions={0} | all-to-all | bytes 393216 | tf_op jit(solution)/shard_map/all_to_all | solution.py:29
  152.1 11.7 %all_to_all.44.parts = bf16[16,48,128]{2,1,0:T(8,128)(2,1)S(1)} all-to-all(bf16[16,48,128]{2,1,0:T(8,128)(2,1)S(1)} %shard_map.92), channel_id=1, replica_groups=mesh['y'=8,'xl'=2,'core'=2,'xh'=2,'z'=8] {'y','xl'}, dimensions={0} | all-to-all | bytes 393216 | tf_op jit(solution)/shard_map/all_to_all | solution.py:29
  163.9 12.6 %all_to_all.45 = bf16[16,48,128]{2,1,0:T(8,128)(2,1)S(1)} all-to-all(bf16[16,48,128]{2,1,0:T(8,128)(2,1)S(1)} %shard_map.93), channel_id=1, replica_groups=mesh['y'=8,'xl'=2,'core'=2,'xh'=2,'z'=8] {'xh','z'}, dimensions={0} | all-to-all | bytes 393216 | tf_op jit(solution)/shard_map/all_to_all | solution.py:29
  176.5 1.9 %collective-permute-start.5 = (bf16[768,128]{1,0:T(8,128)(2,1)S(1)}, bf16[768,128]{1,0:T(8,128)(2,1)S(1)}, u32[]{:S(2)}, u32[]{:S(2)}) collective-permute-start(bf16[768,128]{1,0:T(8,128)(2,1)S(1)} %bitcast.6), channel_id=1, source_target_pairs={{0,16},{16,0},{1,17},{17,1},{2,18},{18,2},{3,19},{19,3},{4,20},{20... | collective-permute-start | bytes 589832 | tf_op jit(solution)/shard_map/ppermute | solution.py:25
  178.4 2.4 %collective-permute-start.4 = (bf16[2,128,128]{2,1,0:T(8,128)(2,1)S(1)}, bf16[2,128,128]{2,1,0:T(8,128)(2,1)S(1)}, u32[]{:S(2)}, u32[]{:S(2)}) collective-permute-start(bf16[2,128,128]{2,1,0:T(8,128)(2,1)S(1)} %get-tuple-element.55), channel_id=1, source_target_pairs={{0,16},{16,0},{1,17},{17,1},{2,18},{18,2},{3,19},{19,3},{4,20},{20... | collective-permute-start | bytes 196616 | tf_op jit(solution)/shard_map/ppermute | solution.py:25
  180.8 0.9 collective-permute-done.4.late
  181.7 0.0 copy-done
  181.7 1.0 shard_map.91
  182.7 0.0 collective-permute-done.5
  182.7 1.0 fusion
  (4 shorter events, 0.1 us)
Async XLA Ops:
  2.1 10.0 %collective-permute-start = (bf16[144,1024]{1,0:T(8,128)(2,1)S(1)}, bf16[144,1024]{1,0:T(8,128)(2,1)S(1)}, u32[]{:S(2)}, u32[]{:S(2)}) collective-permute-start(bf16[144,1024]{1,0:T(8,128)(2,1)S(1)} %get-tuple-element.42), channel_id=1, source_target_pairs={{0,16},{16,0},{1,17},{17,1},{2,18},{18,2},{3,19},{19,3},{4,20},{20... | collective-permute-start | bytes 884744 | tf_op jit(solution)/shard_map/ppermute | solution.py:25
  12.1 37.9 %collective-permute-start.3 = (bf16[96,128,128]{2,1,0:T(8,128)(2,1)}, bf16[96,128,128]{2,1,0:T(8,128)(2,1)}, u32[]{:S(2)}, u32[]{:S(2)}) collective-permute-start(bf16[96,128,128]{2,1,0:T(8,128)(2,1)} %own_in.1), channel_id=1, source_target_pairs={{0,16},{16,0},{1,17},{17,1},{2,18},{18,2},{3,19},{19,3},{4,20},{20... | collective-permute-start | bytes 9437192 | tf_op jit(solution)/shard_map/ppermute | solution.py:25
  14.6 17.8 %collective-permute-start.1 = (bf16[128,128]{1,0:T(8,128)(2,1)S(1)}, bf16[128,128]{1,0:T(8,128)(2,1)S(1)}, u32[]{:S(2)}, u32[]{:S(2)}) collective-permute-start(bf16[128,128]{1,0:T(8,128)(2,1)S(1)} %slice.11), channel_id=1, source_target_pairs={{0,16},{1,17},{2,18},{3,19},{4,20},{5,21},{6,22},{7,23},{8,24},{9,... | collective-permute-start | bytes 98312 | tf_op jit(solution)/shard_map/ppermute | solution.py:69
  47.7 10.1 %collective-permute-start.2 = (bf16[8,2,128,128]{3,2,1,0:T(8,128)(2,1)}, bf16[8,2,128,128]{3,2,1,0:T(8,128)(2,1)S(1)}, u32[]{:S(2)}, u32[]{:S(2)}) collective-permute-start(bf16[8,2,128,128]{3,2,1,0:T(8,128)(2,1)} %get-tuple-element.60.panels_in), channel_id=1, source_target_pairs={{0,32},{32,0},{1,33},{33,1},{2,34},{34,2},{3,35},{35,3},{4,36},{36... | collective-permute-start | bytes 1572872 | tf_op jit(solution)/shard_map/ppermute | solution.py:72
  113.3 25.2 %copy-start.1 = (bf16[128,768]{1,0:T(8,128)(2,1)S(1)}, bf16[128,768]{1,0:T(8,128)(2,1)}, u32[]{:S(2)}) copy-start(bf16[128,768]{1,0:T(8,128)(2,1)} %features.3) | copy-start | bytes 589828
  113.3 25.2 %copy-start.2 = (s32[1,128]{1,0:T(1,128)S(1)}, s32[1,128]{1,0:T(1,128)}, u32[]{:S(2)}) copy-start(s32[1,128]{1,0:T(1,128)} %order.1) | copy-start | bytes 1540
  115.8 65.9 %copy-start = (bf16[768,256]{1,0:T(8,128)(2,1)S(1)}, bf16[768,256]{1,0:T(8,128)(2,1)}, u32[]{:S(2)}) copy-start(bf16[768,256]{1,0:T(8,128)(2,1)} %weight.1) | copy-start | bytes 1179652
  176.5 6.2 %collective-permute-start.5 = (bf16[768,128]{1,0:T(8,128)(2,1)S(1)}, bf16[768,128]{1,0:T(8,128)(2,1)S(1)}, u32[]{:S(2)}, u32[]{:S(2)}) collective-permute-start(bf16[768,128]{1,0:T(8,128)(2,1)S(1)} %bitcast.6), channel_id=1, source_target_pairs={{0,16},{16,0},{1,17},{17,1},{2,18},{18,2},{3,19},{19,3},{4,20},{20... | collective-permute-start | bytes 589832 | tf_op jit(solution)/shard_map/ppermute | solution.py:25
  178.4 3.3 %collective-permute-start.4 = (bf16[2,128,128]{2,1,0:T(8,128)(2,1)S(1)}, bf16[2,128,128]{2,1,0:T(8,128)(2,1)S(1)}, u32[]{:S(2)}, u32[]{:S(2)}) collective-permute-start(bf16[2,128,128]{2,1,0:T(8,128)(2,1)S(1)} %get-tuple-element.55), channel_id=1, source_target_pairs={{0,16},{16,0},{1,17},{17,1},{2,18},{18,2},{3,19},{19,3},{4,20},{20... | collective-permute-start | bytes 196616 | tf_op jit(solution)/shard_map/ppermute | solution.py:25
